TPU v7x, 512 devices: a whole 4x4x16 slice. The times are simulated.
512 devices in a mesh: dp: 32 (over y, z_lo), height: 16 (over x, z_hi, core).
Axes of the slice: x: 4, y: 4, z: 16 (z_hi: 2, z_lo: 8; z = z_hi * 8 + z_lo), core: 2. Of those that a mesh axis runs over, the one named last changes fastest.
Arguments:
- frames: bfloat16 [32, 256, 128, 128], P('dp', 'height'), may hold values from -6 to 6
- cotangent: bfloat16 [32, 256, 128, 128], P('dp', 'height'), may hold values from -6 to 6
- w_in: bfloat16 [3, 3, 128, 128], P(None, None, 'dp'), may hold values from -0.1875 to 0.1875
- w_down: bfloat16 [3, 3, 128, 256], P(None, None, 'dp'), may hold values from -0.1875 to 0.1875
- w_up: bfloat16 [3, 3, 256, 128], P(None, None, 'dp'), may hold values from -0.25 to 0.25
Outputs:
- output: bfloat16 [32, 256, 128, 128], P('dp', 'height')
- input_grad: bfloat16 [32, 256, 128, 128], P('dp', 'height')
- grad_in: float32 [3, 3, 128, 128], P(None, None, 'dp', 'height')
- grad_down: float32 [3, 3, 128, 256], P(None, None, 'dp', 'height')
- grad_up: float32 [3, 3, 256, 128], P(None, None, 'dp', 'height')
All inputs are finite; a program needn't handle non-finite values.
Results may differ from a plain program's by a relative error of at most 0.0055.
Values may be sent and summed in bfloat16 or wider, within the bound.
A program may use at most 64 MiB of HBM per device.

v0:
```python
import math

import jax
import jax.numpy as jnp
from jax import lax
from jax.sharding import PartitionSpec as P

LAYOUT = ("NHWC", "HWIO", "NHWC")
FLAT = ((0, 0), (0, 0))
SIDE_PAD = ((0, 0), (0, 0), (1, 1), (0, 0))
LEFT_PAD = ((0, 0), (0, 0), (1, 0), (0, 0))


def padded(cells, sides, width):
    for axis, dim in sides:
        count = lax.axis_size(axis)
        ends = count - 1
        head = lax.slice_in_dim(cells, 0, width, axis=dim)
        tail = lax.slice_in_dim(cells, cells.shape[dim] - width, cells.shape[dim], axis=dim)
        cells = jnp.concatenate(
            [
                lax.ppermute(tail, axis, [(i, (i + 1) % count) for i in range(ends)]),
                cells,
                lax.ppermute(head, axis, [((i + 1) % count, i) for i in range(ends)]),
            ],
            axis=dim,
        )
    return cells


def from_behind(shard, axis, by):
    devices = lax.axis_size(axis)
    pairs = [(i, i + by) for i in range(devices) if 0 <= i + by < devices]
    return lax.ppermute(shard, axis, pairs)


def conv_plain(inputs, kernel, stride, padding, dilate):
    return lax.conv_general_dilated(
        inputs,
        kernel,
        (stride, stride),
        padding,
        lhs_dilation=(dilate, dilate),
        dimension_numbers=LAYOUT,
        preferred_element_type=jnp.float32,
    )


def flipped(kernel):
    return jnp.transpose(kernel[::-1, ::-1], (0, 1, 3, 2))


def silu_slope(pre_act):
    sigmoid = jax.nn.sigmoid(pre_act)
    return sigmoid * (1.0 + pre_act * (1.0 - sigmoid))


def kernel_grad(source, cotangent_part, stride):
    rows_out, cols_out = (cotangent_part.shape[1], cotangent_part.shape[2])
    flat_cotangent = cotangent_part.reshape(-1, cotangent_part.shape[3])
    tap_list = []
    for row_tap in range(3):
        for col_tap in range(3):
            window = source[
                :,
                row_tap : row_tap + stride * (rows_out - 1) + 1 : stride,
                col_tap : col_tap + stride * (cols_out - 1) + 1 : stride,
                :,
            ]
            tap_list.append(
                jnp.dot(
                    window.reshape(-1, source.shape[3]).T,
                    flat_cotangent,
                    preferred_element_type=jnp.float32,
                )
            )
    return jnp.stack(tap_list).reshape(3, 3, source.shape[3], cotangent_part.shape[3])


def on_device(frames, cotangent, w_in, w_down, w_up):
    full_in = lax.all_gather(w_in, "dp", axis=2, tiled=True)
    halo_in = padded(frames, (("height", 1),), 1)
    padded_in = jnp.pad(halo_in, SIDE_PAD)
    pre_fine = conv_plain(padded_in, full_in, 1, FLAT, 1)
    hidden = jax.nn.silu(pre_fine).astype(jnp.bfloat16)
    full_down = lax.all_gather(w_down, "dp", axis=2, tiled=True)
    above_row = from_behind(hidden[:, -1:], "height", 1)
    padded_hidden = jnp.pad(jnp.concatenate([above_row, hidden], 1), LEFT_PAD)
    pre_coarse = conv_plain(padded_hidden, full_down, 2, FLAT, 1)
    coarse = jax.nn.silu(pre_coarse).astype(jnp.bfloat16)
    full_up = lax.all_gather(w_up, "dp", axis=2, tiled=True)
    below_row = from_behind(coarse[:, :1], "height", -1)
    upsampled = conv_plain(jnp.concatenate([coarse, below_row], 1), full_up, 1, ((1, 0), (1, 2)), 2)
    output = (frames.astype(jnp.float32) + upsampled).astype(jnp.bfloat16)
    cotangent_above = from_behind(cotangent[:, -1:], "height", 1)
    padded_cotangent = jnp.pad(jnp.concatenate([cotangent_above, cotangent], 1), LEFT_PAD)
    back_up = lax.all_gather(w_up, "dp", axis=2, tiled=True)
    grad_coarse = conv_plain(padded_cotangent, flipped(back_up), 2, FLAT, 1)
    grad_pre_coarse = (grad_coarse * silu_slope(pre_coarse)).astype(jnp.bfloat16)
    back_down = lax.all_gather(w_down, "dp", axis=2, tiled=True)
    grad_below = from_behind(grad_pre_coarse[:, :1], "height", -1)
    grad_hidden = conv_plain(
        jnp.concatenate([grad_pre_coarse, grad_below], 1),
        flipped(back_down),
        1,
        ((1, 0), (1, 2)),
        2,
    )
    grad_pre_fine = (grad_hidden * silu_slope(pre_fine)).astype(jnp.bfloat16)
    back_in = lax.all_gather(w_in, "dp", axis=2, tiled=True)
    halo_grad = padded(grad_pre_fine, (("height", 1),), 1)
    grad_input = conv_plain(jnp.pad(halo_grad, SIDE_PAD), flipped(back_in), 1, FLAT, 1)
    input_grad = (cotangent.astype(jnp.float32) + grad_input).astype(jnp.bfloat16)
    grad_first = kernel_grad(padded_in, grad_pre_fine, 1)
    grad_second = kernel_grad(padded_hidden, grad_pre_coarse, 2)
    grad_third = flipped(kernel_grad(padded_cotangent, coarse, 2))
    shares = (
        lax.psum_scatter(grad_first, "dp", scatter_dimension=2, tiled=True),
        lax.psum_scatter(grad_second, "dp", scatter_dimension=2, tiled=True),
        lax.psum_scatter(grad_third, "dp", scatter_dimension=2, tiled=True),
    )
    shares = (
        lax.psum_scatter(shares[0], "height", scatter_dimension=3, tiled=True),
        lax.psum_scatter(shares[1], "height", scatter_dimension=3, tiled=True),
        lax.psum_scatter(shares[2], "height", scatter_dimension=3, tiled=True),
    )
    pixel_count = (
        lax.axis_size("dp")
        * frames.shape[0]
        * frames.shape[1]
        * lax.axis_size("height")
        * frames.shape[2]
    )
    factor = 1.0 / math.sqrt(pixel_count)
    return (output, input_grad, shares[0] * factor, shares[1] * factor, shares[2] * factor)


def solution(mesh):
    in_specs = (
        P("dp", "height", None, None),
        P("dp", "height", None, None),
        P(None, None, "dp", None),
        P(None, None, "dp", None),
        P(None, None, "dp", None),
    )
    out_specs = (
        P("dp", "height", None, None),
        P("dp", "height", None, None),
        P(None, None, "dp", "height"),
        P(None, None, "dp", "height"),
        P(None, None, "dp", "height"),
    )
    return jax.shard_map(
        on_device, mesh=mesh, in_specs=in_specs, out_specs=out_specs, check_vma=False
    )
```

profile of v0, /device:TPU:1, one launch (start us, length us, event | category | flops | bytes accessed | tf_op | source)
XLA Modules:
  0.0 1389.5 jit_solution(11679562082813202536)
XLA Ops:
  7.2 1.4 copy.61
  8.6 8.8 collective-permute-start.1
  17.4 10.0 collective-permute-start
  28.2 2.4 collective-permute-start.4
  30.6 116.4 %all_gather.14 = bf16[3,3,256,128]{3,2,1,0:T(8,128)(2,1)} all-gather(bf16[3,3,8,128]{3,2,1,0:T(8,128)(2,1)S(1)} %copy-done.32), channel_id=1, replica_groups=mesh['dp'=32,'height'=16] {'dp'}, dimensions={2}, use_global_device_ids=true | all-gather | bytes 608256 | tf_op jit(solution)/shard_map/all_gather | solution.py:91
  147.0 110.0 %all_gather.13 = bf16[3,3,128,256]{3,1,0,2:T(4,128)(2,1)} all-gather(bf16[3,3,4,256]{3,1,0,2:T(4,128)(2,1)S(1)} %copy.74), channel_id=1, replica_groups=mesh['dp'=32,'height'=16] {'dp'}, dimensions={2}, use_global_device_ids=true | all-gather | bytes 608256 | tf_op jit(solution)/shard_map/all_gather | solution.py:86
  257.0 101.9 %all_gather.12 = bf16[3,3,128,128]{3,1,0,2:T(4,128)(2,1)S(1)} all-gather(bf16[3,3,4,128]{3,1,0,2:T(4,128)(2,1)S(1)} %copy.67), channel_id=1, replica_groups=mesh['dp'=32,'height'=16] {'dp'}, dimensions={2}, use_global_device_ids=true | all-gather | bytes 304128 | tf_op jit(solution)/shard_map/all_gather | solution.py:81
  358.9 1.3 dynamic-slice
  360.9 0.9 pad_maximum_fusion
  363.3 2.7 add_multiply_fusion
  366.7 51.3 %collective-permute-start.2 = (bf16[1,1,128,128]{3,2,1,0:T(8,128)(2,1)}, bf16[1,1,128,128]{3,2,1,0:T(8,128)(2,1)}, u32[]{:S(2)}, u32[]{:S(2)}) collective-permute-start(bf16[1,1,128,128]{3,2,1,0:T(8,128)(2,1)} %slice.168), channel_id=1, source_target_pairs={{0,1},{1,2},{2,3},{3,4},{4,5},{5,6},{6,7},{7,8},{8,9},{9,10},{10,1... | collective-permute-start | bytes 98312 | tf_op jit(solution)/shard_map/ppermute | solution.py:34
  418.3 2.5 slice.133
  420.8 2.5 slice.134
  423.3 2.5 slice.135
  425.8 2.5 slice.136
  428.3 2.5 slice.137
  430.8 2.5 slice.138
  435.0 0.9 copy.253
  437.7 1.1 pad.25
  441.3 1.3 multiply_convert_fusion.1
  444.1 2.5 slice.124
  446.6 2.5 slice.125
  449.1 2.5 slice.126
  451.6 2.5 slice.127
  456.5 2.2 collective-permute-start.5
  458.8 1.1 fusion.25
  459.9 1.1 fusion.24
  462.7 1.1 fusion.16
  463.9 6.7 collective-permute-done.5
  471.3 2.8 fusion.5
  480.7 0.9 fusion.15
  485.1 0.9 fusion.10
  487.7 1.6 copy.105
  489.3 425.5 %all-reduce.11.cloned.1.call-done = (f32[3,3,128,128]{3,2,1,0:T(8,128)}, f32[3,3,128,256]{3,2,1,0:T(8,128)}) async-done(((f32[3,3,128,128]{3,2,1,0:T(8,128)}, f32[3,3,128,256]{3,2,1,0:T(8,128)}), (f32[3,3,128,128]{3,2,1,0:T(8,128)}, f32[3,3,128,256]{3,2,1,0:T(8,128)})) %all-reduce.11.cloned.1.call-update) | async-done | bytes 1769488
  914.9 0.9 constant_dynamic-slice_fusion
  916.5 1.3 reshape.326
  917.9 1.2 reverse_bitcast_fusion
  919.9 22.8 %collective-permute-start.3 = (bf16[1,1,64,256]{3,2,1,0:T(8,128)(2,1)S(1)}, bf16[1,1,64,256]{3,2,1,0:T(8,128)(2,1)S(1)}, u32[]{:S(2)}, u32[]{:S(2)}) collective-permute-start(bf16[1,1,64,256]{3,2,1,0:T(8,128)(2,1)S(1)} %slice.173), channel_id=1, source_target_pairs={{1,0},{2,1},{3,2},{4,3},{5,4},{6,5},{7,6},{8,7},{9,8},{10,9},{11,1... | collective-permute-start | bytes 98312 | tf_op jit(solution)/shard_map/ppermute | solution.py:34
  942.8 1.3 dynamic-slice.2
  944.7 9.2 collective-permute-done.3
  957.2 2.1 collective-permute-start.7
  959.3 12.6 collective-permute-start.6
  972.4 0.9 copy.106
  974.8 1.5 convolution_select_fusion
  977.7 0.9 copy.107
  979.4 52.7 %reduce-scatter.11.cloned.1.call-done = f32[16,36]{1,0:T(8,128)} async-done(((f32[256,36]{1,0:T(8,128)}), f32[16,36]{1,0:T(8,128)}) %reduce-scatter.11.cloned.1.call-update) | async-done | bytes 2320
  1033.6 211.9 %reduce-scatter.9.cloned.1.call-done = f32[3,3,8,128]{3,2,1,0:T(8,128)} async-done(((f32[3,3,256,128]{3,2,1,0:T(8,128)}), f32[3,3,8,128]{3,2,1,0:T(8,128)}) %reduce-scatter.9.cloned.1.call-update) | async-done | bytes 36880 | tf_op jit(solution)/shard_map/reduce_scatter | solution.py:120
  1245.6 136.0 %all-reduce.8 = (f32[3,3,4,128]{3,2,1,0:T(4,128)S(1)}, f32[3,3,8,128]{3,2,1,0:T(8,128)S(1)}) all-reduce(f32[3,3,4,128]{3,2,1,0:T(4,128)S(1)} %constant_dynamic-slice_fusion.1, f32[3,3,8,128]{3,2,1,0:T(8,128)} %reduce-scatter.9.cloned.1.call-done), channel_id=3, replica_groups=mesh['dp'=32,'height'=16] {'height'}, use_global_device_ids=true, to_apply=%region_1.2.clone | all-reduce | flops 13824 | bytes 110592
  (200 shorter events, 38.6 us)
Async XLA Ops:
  7.2 23.4 %copy-start.32 = (bf16[3,3,8,128]{3,2,1,0:T(8,128)(2,1)S(1)}, bf16[3,3,8,128]{3,2,1,0:T(8,128)(2,1)}, u32[]{:S(2)}) copy-start(bf16[3,3,8,128]{3,2,1,0:T(8,128)(2,1)} %param.9) | copy-start | bytes 55300
  7.2 139.8 %copy-start.33 = (bf16[3,3,4,256]{3,2,1,0:T(4,128)(2,1)S(1)}, bf16[3,3,4,256]{3,2,1,0:T(4,128)(2,1)}, u32[]{:S(2)}) copy-start(bf16[3,3,4,256]{3,2,1,0:T(4,128)(2,1)} %param.8) | copy-start | bytes 55300
  7.2 249.8 %copy-start.34 = (bf16[3,3,4,128]{3,2,1,0:T(4,128)(2,1)S(1)}, bf16[3,3,4,128]{3,2,1,0:T(4,128)(2,1)}, u32[]{:S(2)}) copy-start(bf16[3,3,4,128]{3,2,1,0:T(4,128)(2,1)} %param.7) | copy-start | bytes 27652
  7.2 907.7 %all-reduce.11.cloned.1.call-start = ((), (), s32[]{:S(2)}) async-start(), calls=%async_computation.4 | async-start | bytes 3538944
  8.6 352.2 %collective-permute-start.1 = (bf16[1,1,128,128]{2,3,1,0:T(8,128)(2,1)S(1)}, bf16[1,1,128,128]{2,3,1,0:T(8,128)(2,1)S(1)}, u32[]{:S(2)}, u32[]{:S(2)}) collective-permute-start(bf16[1,1,128,128]{2,3,1,0:T(8,128)(2,1)S(1)} %get-tuple-element.28), channel_id=1, source_target_pairs={{1,0},{2,1},{3,2},{4,3},{5,4},{6,5},{7,6},{8,7},{9,8},{10,9},{11,1... | collective-permute-start | bytes 98312 | tf_op jit(solution)/shard_map/ppermute | solution.py:24
  17.4 343.5 %collective-permute-start = (bf16[1,1,128,128]{2,3,1,0:T(8,128)(2,1)S(1)}, bf16[1,1,128,128]{2,3,1,0:T(8,128)(2,1)S(1)}, u32[]{:S(2)}, u32[]{:S(2)}) collective-permute-start(bf16[1,1,128,128]{2,3,1,0:T(8,128)(2,1)S(1)} %get-tuple-element.27), channel_id=1, source_target_pairs={{0,1},{1,2},{2,3},{3,4},{4,5},{5,6},{6,7},{7,8},{8,9},{9,10},{10,1... | collective-permute-start | bytes 98312 | tf_op jit(solution)/shard_map/ppermute | solution.py:22
  28.2 389.8 %collective-permute-start.4 = (bf16[1,1,128,128]{3,2,1,0:T(8,128)(2,1)S(1)}, bf16[1,1,128,128]{3,2,1,0:T(8,128)(2,1)S(1)}, u32[]{:S(2)}, u32[]{:S(2)}) collective-permute-start(bf16[1,1,128,128]{3,2,1,0:T(8,128)(2,1)S(1)} %slice.112), channel_id=1, source_target_pairs={{0,1},{1,2},{2,3},{3,4},{4,5},{5,6},{6,7},{7,8},{8,9},{9,10},{10,1... | collective-permute-start | bytes 98312 | tf_op jit(solution)/shard_map/ppermute | solution.py:34
  358.9 3.8 copy-start.25
  360.9 1.3 copy-start.30
  363.3 54.7 %copy-start = (bf16[1,16,128,128]{3,2,1,0:T(8,128)(2,1)S(1)}, bf16[1,16,128,128]{3,2,1,0:T(8,128)(2,1)}, u32[]{:S(2)}) copy-start(bf16[1,16,128,128]{3,2,1,0:T(8,128)(2,1)} %param.6) | copy-start | bytes 1572868
  366.7 72.2 %collective-permute-start.2 = (bf16[1,1,128,128]{3,2,1,0:T(8,128)(2,1)}, bf16[1,1,128,128]{3,2,1,0:T(8,128)(2,1)}, u32[]{:S(2)}, u32[]{:S(2)}) collective-permute-start(bf16[1,1,128,128]{3,2,1,0:T(8,128)(2,1)} %slice.168), channel_id=1, source_target_pairs={{0,1},{1,2},{2,3},{3,4},{4,5},{5,6},{6,7},{7,8},{8,9},{9,10},{10,1... | collective-permute-start | bytes 98312 | tf_op jit(solution)/shard_map/ppermute | solution.py:34
  434.9 1.4 copy-start.8
  437.0 1.8 copy-start.10
  437.7 1.2 copy-start.2
  440.1 1.1 copy-start.9
  441.3 1.3 copy-start.11
  441.3 1.3 copy-start.15
  441.3 1.3 copy-start.29
  443.2 0.7 copy-start.28
  444.1 12.2 copy-start.27
  454.1 2.3 slice-start
  456.4 4.6 copy-start.24
  456.4 4.9 copy-start.23
  456.5 14.1 %collective-permute-start.5 = (bf16[1,1,64,256]{3,2,1,0:T(8,128)(2,1)S(1)}, bf16[1,1,64,256]{3,2,1,0:T(8,128)(2,1)S(1)}, u32[]{:S(2)}, u32[]{:S(2)}) collective-permute-start(bf16[1,1,64,256]{3,2,1,0:T(8,128)(2,1)S(1)} %slice.179), channel_id=1, source_target_pairs={{1,0},{2,1},{3,2},{4,3},{5,4},{6,5},{7,6},{8,7},{9,8},{10,9},{11,1... | collective-permute-start | bytes 98312 | tf_op jit(solution)/shard_map/ppermute | solution.py:34
  461.8 1.0 copy-start.22
  462.7 8.1 copy-start.7
  470.6 0.7 copy-start.36
  474.1 0.8 copy-start.12
  474.1 1.3 copy-start.13
  474.9 0.8 copy-start.31
  475.0 3.6 copy-start.3
  476.1 1.0 copy-start.5
  478.9 0.8 copy-start.14
  479.8 0.9 copy-start.21
  479.8 1.8 copy-start.20
  479.8 2.7 copy-start.19
  479.8 3.5 copy-start.18
  479.8 4.4 copy-start.17
  479.8 552.3 %reduce-scatter.11.cloned.1.call-start = ((), (), s32[]{:S(2)}) async-start(), calls=%async_computation.3 | async-start | bytes 139264
  917.8 327.8 %reduce-scatter.9.cloned.1.call-start = ((), (), s32[]{:S(2)}) async-start(), calls=%async_computation.2 | async-start | bytes 1216512 | tf_op jit(solution)/shard_map/reduce_scatter | solution.py:120
  919.9 34.1 %collective-permute-start.3 = (bf16[1,1,64,256]{3,2,1,0:T(8,128)(2,1)S(1)}, bf16[1,1,64,256]{3,2,1,0:T(8,128)(2,1)S(1)}, u32[]{:S(2)}, u32[]{:S(2)}) collective-permute-start(bf16[1,1,64,256]{3,2,1,0:T(8,128)(2,1)S(1)} %slice.173), channel_id=1, source_target_pairs={{1,0},{2,1},{3,2},{4,3},{5,4},{6,5},{7,6},{8,7},{9,8},{10,9},{11,1... | collective-permute-start | bytes 98312 | tf_op jit(solution)/shard_map/ppermute | solution.py:34
  954.0 1.1 copy-start.16
  955.9 16.0 %copy-start.6 = (bf16[1,16,128,128]{3,2,1,0:T(8,128)(2,1)S(1)}, bf16[1,16,128,128]{3,2,1,0:T(8,128)(2,1)}, u32[]{:S(2)}) copy-start(bf16[1,16,128,128]{3,2,1,0:T(8,128)(2,1)} %param.5) | copy-start | bytes 1572868
  957.2 15.1 %copy-start.4 = (bf16[16,1,128,128]{3,0,2,1:T(8,128)(2,1)S(1)}, bf16[16,1,128,128]{3,0,2,1:T(8,128)(2,1)}, u32[]{:S(2)}) copy-start(bf16[16,1,128,128]{3,0,2,1:T(8,128)(2,1)} %copy-done.3) | copy-start | bytes 1572868
  957.2 16.2 %collective-permute-start.7 = (bf16[1,1,128,128]{3,2,1,0:T(8,128)(2,1)S(1)}, bf16[1,1,128,128]{3,2,1,0:T(8,128)(2,1)S(1)}, u32[]{:S(2)}, u32[]{:S(2)}) collective-permute-start(bf16[1,1,128,128]{3,2,1,0:T(8,128)(2,1)S(1)} %slice.185), channel_id=1, source_target_pairs={{1,0},{2,1},{3,2},{4,3},{5,4},{6,5},{7,6},{8,7},{9,8},{10,9},{11,1... | collective-permute-start | bytes 98312 | tf_op jit(solution)/shard_map/ppermute | solution.py:24
  959.3 14.0 %collective-permute-start.6 = (bf16[1,1,128,128]{3,2,1,0:T(8,128)(2,1)S(1)}, bf16[1,1,128,128]{3,2,1,0:T(8,128)(2,1)S(1)}, u32[]{:S(2)}, u32[]{:S(2)}) collective-permute-start(bf16[1,1,128,128]{3,2,1,0:T(8,128)(2,1)S(1)} %slice.182), channel_id=1, source_target_pairs={{0,1},{1,2},{2,3},{3,4},{4,5},{5,6},{6,7},{7,8},{8,9},{9,10},{10,1... | collective-permute-start | bytes 98312 | tf_op jit(solution)/shard_map/ppermute | solution.py:22
  973.8 1.0 copy-start.26
  976.3 1.0 copy-start.1
  (2 other events, 1.4 us)
Sparse Core Ops, SparseCore 0:
  479.9 434.9 all-reduce.10
  920.1 111.8 reduce-scatter.10
  1034.9 210.6 reduce-scatter.8
where the time goes:
time: 1400 us; the launch traced here: 1390 us
  waiting for transfers between devices  706 us (50%)
  blocking collectives  464 us (33%)
  starting transfers between devices  112 us (8%)
  local copies, waits for them, and re-layouts  61.1 us (4%)
  matrix products  24.9 us (2%)
  between operations  16.2 us (1%)
    unnamed x5, waiting for transfers between devices  478 us
    reduce_scatter x1, waiting for transfers between devices, on_device(): lax.psum_scatter(grad_third, 'dp', scatter_dimension=2, tiled=True)  212 us
    unnamed x1, blocking collectives  136 us
    all_gather x1, blocking collectives, on_device(): full_up = lax.all_gather(w_up, 'dp', axis=2, tiled=True)  116 us
    all_gather x1, blocking collectives, on_device(): full_down = lax.all_gather(w_down, 'dp', axis=2, tiled=True)  110 us
    all_gather x1, blocking collectives, on_device(): full_in = lax.all_gather(w_in, 'dp', axis=2, tiled=True)  102 us
    ppermute x4, starting transfers between devices, from_behind(): return lax.ppermute(shard, axis, pairs)  78.7 us
    slice x18, local copies, waits for them, and re-layouts, kernel_grad(): source[:, row_tap:row_tap + stride * (rows_out - 1) + 1:stride, col_tap:c...  28.8 us
  transfers between devices with their start and end apart: 11, of which 5 were waited for; matrix products, arithmetic and copies ran while one was open for 4% of the time, Pallas kernels for 0%

commit v1 on v0

v1 whole, which is shorter than its diff:
```python
import functools
import math

import jax
import jax.numpy as jnp
from jax import lax
from jax.experimental import pallas as pl
from jax.experimental.pallas import tpu as pltpu
from jax.sharding import PartitionSpec as P

F32, BF16 = jnp.float32, jnp.bfloat16
MESH = pl.DeviceIdType.MESH

PACK = 208
DOWN_AT = 48
UP_AT = 128
HOPS = (1, -1, 2, -2, 3, -3, 4)
JOBS = ((0, 48, "x"), (48, 80, "y"), (128, 80, "x"))
IN, DOWN, UP = 0, 1, 2


def place():
    d = lax.axis_index("dp")
    h = lax.axis_index("height")
    z = lax.rem(lax.div(h, 2), 2) * 8 + lax.rem(d, 8)
    return lax.div(h, 4), lax.div(d, 8), z, lax.rem(h, 2)


def device(x, y, z, core):
    return (y * 8 + lax.rem(z, 8), x * 4 + lax.div(z, 8) * 2 + core)


def on_ring(position, by, size):
    return lax.rem(position + by + size, size)


def remote(source, target, send, recv, where):
    return pltpu.make_async_remote_copy(
        src_ref=source, dst_ref=target, send_sem=send, recv_sem=recv, device_id=where, device_id_type=MESH
    )


def when(condition, action):
    @pl.when(condition)
    def _():
        action()


def every(copies, act):
    for copy in copies:
        getattr(copy, act)()


def spread_columns(rows, first, wide, stacked, slots):
    count = rows.shape[0]
    wide[pl.ds(first, count), 8:136] = rows[...].astype(F32)
    for row in range(first, first + count):
        target = stacked.at[row] if len(stacked.shape) == 3 else stacked.at[row // 2, row % 2]
        for slot in range(slots):
            target[:, slot * 128 : slot * 128 + 128] = wide[row, pl.ds(7 + slot, 64, stride=2), :].astype(BF16)


def matmul(left, right):
    return lax.dot_general(left, right, (((1,), (0,)), ((), ())), preferred_element_type=F32)


def matmul_t(left, right):
    return lax.dot_general(left, right, (((1,), (1,)), ((), ())), preferred_element_type=F32)


def flat(cells):
    return cells.reshape(cells.shape[0] * cells.shape[1], cells.shape[2])


def shuffle(taps, channels, pitch, transposed):
    shards = 16 // channels
    dims = (shards * pitch, taps * 16) if transposed else (taps * 16, shards * pitch)
    row = lax.broadcasted_iota(jnp.int32, dims, 1 if transposed else 0)
    column = lax.broadcasted_iota(jnp.int32, dims, 0 if transposed else 1)
    bits = channels.bit_length() - 1
    wanted = ((row & 15) >> bits) * pitch + (row >> 4) * channels + (row & (channels - 1))
    return (column == wanted).astype(F32).astype(BF16)


def unpack_in(full, win):
    order = shuffle(9, 4, 48, False)
    for group in range(8):
        k, y = 4 * (group % 2), group // 2
        rows = matmul(order, full[k : k + 4, y, 0:DOWN_AT].reshape(192, 128)).astype(BF16)
        win[:, 16 * group : 16 * group + 16] = rows.reshape(9, 16, 128)


def unpack_down(full, wdn):
    order = shuffle(18, 4, 80, False)
    for group in range(8):
        k, y = 4 * (group % 2), group // 2
        rows = matmul(order, full[k : k + 4, y, DOWN_AT:UP_AT].reshape(320, 128)).astype(BF16)
        wdn[:, 16 * group : 16 * group + 16, 0:128] = rows[0:144].reshape(9, 16, 128)
        wdn[:, 16 * group : 16 * group + 16, 128:256] = rows[144:288].reshape(9, 16, 128)


def unpack_up(full, wup):
    order = shuffle(9, 8, 80, False)
    for group in range(16):
        k, y = 2 * (group % 4), group // 4
        rows = matmul(order, full[k : k + 2, y, UP_AT:PACK].reshape(160, 128)).astype(BF16)
        wup[:, 16 * group : 16 * group + 16] = rows.reshape(9, 16, 128)


def pack_in(parts, sin):
    order = shuffle(9, 4, 48, True)
    for group in range(8):
        k, y = 4 * (group % 2), group // 2
        rows = matmul(order, sin[:, 16 * group : 16 * group + 16].reshape(144, 128)).astype(BF16)
        parts[k : k + 4, y, 0:DOWN_AT] = rows.reshape(4, 48, 128)


def pack_down(parts, sdn):
    order = shuffle(18, 4, 80, True)
    for group in range(8):
        k, y = 4 * (group % 2), group // 2
        halves = [sdn[:, 16 * group : 16 * group + 16, at : at + 128].reshape(144, 128) for at in (0, 128)]
        rows = matmul(order, jnp.concatenate(halves, axis=0)).astype(BF16)
        parts[k : k + 4, y, DOWN_AT:UP_AT] = rows.reshape(4, 80, 128)


def pack_up(parts, sup):
    order = shuffle(9, 8, 80, True)
    for group in range(16):
        k, y = 2 * (group % 4), group // 4
        rows = matmul(order, sup[:, 16 * group : 16 * group + 16].reshape(144, 128)).astype(BF16)
        parts[k : k + 2, y, UP_AT:PACK] = rows.reshape(2, 80, 128)


def stack_in(win, fine, back_fine):
    blank = jnp.zeros((128, 128), BF16)
    for j in range(3):
        for slot in range(4):
            at = slice(slot * 128, slot * 128 + 128)
            fine[j, at, 0:128] = win[3 * j + slot] if slot < 3 else blank
            fine[j, at, 128:256] = win[3 * j + slot - 1] if slot > 0 else blank
            back_fine[j, 0:128, at] = win[3 * (2 - j) + 2 - slot] if slot < 3 else blank
            back_fine[j, 128:256, at] = win[3 * (2 - j) + 3 - slot] if slot > 0 else blank


def stack_down(wdn, down, back_down):
    for j in range(3):
        for slot in range(3):
            down[j, slot * 128 : slot * 128 + 128, :] = wdn[3 * j + slot]
        back_down[j, 0:128, 0:256] = wdn[3 * j + 1]
        back_down[j, 0:128, 256:512] = jnp.zeros((128, 256), BF16)
        back_down[j, 128:256, 0:256] = wdn[3 * j + 2]
        back_down[j, 128:256, 256:512] = wdn[3 * j]


def stack_up(wup, up, back_up):
    for j in range(3):
        for slot in range(3):
            back_up[j, :, slot * 128 : slot * 128 + 128] = wup[3 * (2 - j) + 2 - slot]
        up[j, 0:256, 0:128] = wup[3 * j + 1]
        up[j, 0:256, 128:256] = wup[3 * j]
        up[j, 256:512, 0:128] = jnp.zeros((256, 128), BF16)
        up[j, 256:512, 128:256] = wup[3 * j + 2]


def sigmoid(value):
    return 1.0 / (1.0 + jnp.exp(-value))


def pack_own(w_in, w_down, w_up, wide, own):
    wide[...] = jnp.zeros_like(wide)
    for tap in range(9):
        j, l = tap // 3, tap % 3
        wide[4 * tap : 4 * tap + 4] = w_in[j, l].astype(F32)
        for half in range(2):
            at = DOWN_AT + 36 * half + 4 * tap
            wide[at : at + 4] = w_down[j, l, :, 128 * half : 128 * half + 128].astype(F32)
        wide[UP_AT + 8 * tap : UP_AT + 8 * tap + 8] = w_up[j, l].astype(F32)
    own[...] = wide[...].astype(BF16)


def columns(rows, first, width):
    lane = lax.broadcasted_iota(jnp.int32, (128, width), 0)
    wanted = lax.broadcasted_iota(jnp.int32, (128, width), 1) + first
    return lax.dot_general(
        rows, (lane == wanted).astype(F32), (((1,), (0,)), ((), ())),
        precision=lax.Precision.HIGHEST, preferred_element_type=F32,
    )


def take_share(total, band, grad_in, grad_down, grad_up):
    into = columns(total[0:40], band * 8, 8)
    down = columns(total[DOWN_AT : DOWN_AT + 72], lax.rem(band, 8) * 16, 16)
    up = columns(total[UP_AT : UP_AT + 72], band * 8, 8)
    down = jnp.where(band < 8, down[0:36], down[36:72])
    for tap in range(9):
        j, l = tap // 3, tap % 3
        grad_in[j, l] = into[4 * tap : 4 * tap + 4]
        grad_down[j, l] = down[4 * tap : 4 * tap + 4]
        grad_up[j, l] = up[8 * tap : 8 * tap + 8]


class Gather:
    def __init__(self, job, own, full, sems):
        first, count, self.main = JOBS[job]
        self.rows = pl.ds(first, count)
        self.own, self.full = own, full
        self.sems = [sem.at[job] for sem in sems]
        self.x, self.y, self.z, self.core = place()
        self.carried = self.x + 4 * self.core
        self.holder = lax.rem(self.z, 8) == self.carried

    def beside(self, axis, by):
        if axis == "x":
            return device(on_ring(self.x, by, 4), self.y, self.z, self.core)
        return device(self.x, on_ring(self.y, by, 4), self.z, self.core)

    def along_z(self, count=7):
        send, recv = self.sems[0], self.sems[1]
        target = self.full.at[self.carried, self.y, self.rows]
        return [
            remote(
                self.own.at[self.rows], target, send.at[slot], recv.at[0],
                device(self.x, self.y, on_ring(self.z, by, 16), self.core),
            )
            for slot, by in enumerate(HOPS[:count])
        ]

    def light(self):
        send, recv = self.sems[2], self.sems[3]
        axis = "y" if self.main == "x" else "x"
        block = self.full.at[self.carried, self.y, self.rows]
        return [remote(block, block, send.at[by], recv.at[by], self.beside(axis, by)) for by in (1, 3, 2)]

    def piece(self, by, core):
        if self.main == "x":
            return self.full.at[on_ring(self.x, -by, 4) + 4 * core, :, self.rows]
        return self.full.at[pl.ds(4 * core, 4), on_ring(self.y, -by, 4), self.rows]

    def heavy(self, by):
        send, recv = self.sems[4], self.sems[5]
        block = self.piece(0, self.core)
        return remote(block, block, send.at[by], recv.at[by], self.beside(self.main, by))

    def across(self, by):
        send, recv = self.sems[6], self.sems[7]
        block = self.piece(by, self.core)
        other = device(self.x, self.y, self.z, 1 - self.core)
        return remote(block, block, send.at[by], recv.at[by], other)

    def step(self, stage):
        if stage == 0:

            @pl.when(self.holder)
            def _():
                every(self.along_z(), "start")
                self.full[self.carried, self.y, self.rows] = self.own[self.rows]

        if stage == 1:
            when(jnp.logical_not(self.holder), lambda: every(self.along_z(1), "wait_recv"))
            every(self.light(), "start")
        if stage == 2:
            every(self.light(), "wait_recv")
            for by in (1, 3, 2):
                self.heavy(by).start()
            self.across(0).start()
        if stage == 3:
            for by in (1, 3, 2):
                self.heavy(by).wait_recv()
                self.across(by).start()
        if stage == 4:
            for by in range(4):
                self.across(by).wait_recv()
        if stage == 5:
            when(self.holder, lambda: every(self.along_z(), "wait_send"))
            every(self.light(), "wait_send")
            for by in (1, 2, 3):
                self.heavy(by).wait_send()
            for by in range(4):
                self.across(by).wait_send()


class Reduce:
    def __init__(self, job, parts, buffers, sems, scale):
        first, count, self.main = JOBS[job]
        self.rows = pl.ds(first, count)
        self.parts = parts
        (
            self.from_core, self.heavy_out, self.heavy_in, self.sums, self.light_out, self.light_in,
            self.column, self.z_out, self.z_in, self.done, self.total,
        ) = buffers
        self.sems = [sem.at[job] for sem in sems]
        self.scale = scale
        self.x, self.y, self.z, self.core = place()
        self.carried = self.x + 4 * self.core
        self.holder = lax.rem(self.z, 8) == self.carried

    beside = Gather.beside

    def block(self, ref, by, core):
        if self.main == "x":
            return ref.at[on_ring(self.x, by, 4) + 4 * core, :, self.rows]
        return ref.at[pl.ds(4 * core, 4), on_ring(self.y, by, 4), self.rows]

    def across(self, by):
        other = device(self.x, self.y, self.z, 1 - self.core)
        return remote(
            self.block(self.parts, by, 1 - self.core), self.block(self.from_core, by, 0),
            self.sems[0].at[by], self.sems[1].at[by], other,
        )

    def heavy(self, by):
        return remote(
            self.heavy_out.at[by - 1, :, self.rows], self.heavy_in.at[by - 1, :, self.rows],
            self.sems[2].at[by], self.sems[3].at[by], self.beside(self.main, by),
        )

    def light(self, by):
        axis = "y" if self.main == "x" else "x"
        return remote(
            self.light_out.at[by - 1, self.rows], self.light_in.at[by - 1, self.rows],
            self.sems[4].at[by], self.sems[5].at[by], self.beside(axis, by),
        )

    def to_holder(self, at):
        where = self.carried + at
        slot = lax.rem(self.z - where + 31, 16)
        return remote(
            self.z_out.at[self.rows], self.z_in.at[slot, self.rows],
            self.sems[6].at[at // 8], self.sems[7].at[slot], device(self.x, self.y, where, self.core),
        )

    def from_ring(self, slot):
        return remote(
            self.z_out.at[self.rows], self.z_in.at[slot, self.rows],
            self.sems[6].at[0], self.sems[7].at[slot], device(self.x, self.y, self.z, 1 - self.core),
        )

    def spread(self, count=7):
        return [
            remote(
                self.done.at[self.rows], self.total.at[self.rows],
                self.sems[8].at[2 * by + swap], self.sems[9].at[0],
                device(on_ring(self.x, by, 4), self.y, self.z, lax.rem(self.core + swap, 2)),
            )
            for by, swap in ((2, 0), (2, 1), (1, 0), (3, 0), (1, 1), (3, 1), (0, 1))[:count]
        ]

    def both(self, by):
        own = self.block(self.parts, by, self.core)[...].astype(F32)
        return own + self.block(self.from_core, by, 0)[...].astype(F32)

    def step(self, stage):
        rows = self.rows
        if stage == 0:
            for by in (1, 3, 2, 0):
                self.across(by).start()
        if stage == 1:
            for by in (1, 3, 2):
                self.across(by).wait_recv()
                self.heavy_out[by - 1, :, rows] = self.both(by).astype(BF16)
                self.heavy(by).start()
            self.across(0).wait_recv()
            self.sums[:, rows] = self.both(0)
        if stage == 2:
            total = self.sums[:, rows]
            for by in (1, 3, 2):
                self.heavy(by).wait_recv()
                total += self.heavy_in[by - 1, :, rows].astype(F32)
            self.sums[:, rows] = total
            here = self.y if self.main == "x" else self.x
            for by in (1, 3, 2):
                self.light_out[by - 1, rows] = self.sums[on_ring(here, by, 4), rows].astype(BF16)
                self.light(by).start()
            self.column[rows] = self.sums[here, rows]
        if stage == 3:
            total = self.column[rows]
            for by in (1, 3, 2):
                self.light(by).wait_recv()
                total += self.light_in[by - 1, rows].astype(F32)
            self.column[rows] = total
            self.z_out[rows] = total.astype(BF16)
            for at in (0, 8):
                when(self.z != self.carried + at, self.to_holder(at).start)
        if stage == 4:

            @pl.when(self.holder)
            def _():
                total = self.column[rows]
                for slot in range(15):
                    self.from_ring(slot).wait_recv()
                    total += self.z_in[slot, rows].astype(F32)
                total = total * self.scale
                self.done[rows] = total
                every(self.spread(), "start")
                self.total[rows] = total

        if stage == 5:
            when(jnp.logical_not(self.holder), lambda: every(self.spread(1), "wait_recv"))
        if stage == 6:
            for by in range(4):
                self.across(by).wait_send()
            for by in (1, 2, 3):
                self.heavy(by).wait_send()
                self.light(by).wait_send()
            for at in (0, 8):
                when(self.z != self.carried + at, self.to_holder(at).wait_send)
            when(self.holder, lambda: every(self.spread(), "wait_send"))


def greet():
    x, y, z, core = place()
    carried = x + 4 * core
    holder = lax.rem(z, 8) == carried
    row, band = lax.axis_index("dp"), lax.axis_index("height")
    barrier = pltpu.get_barrier_semaphore()

    def signal(where):
        pl.semaphore_signal(barrier, inc=1, device_id=where, device_id_type=MESH)

    signal((row, on_ring(band, -1, 16)))
    signal((row, on_ring(band, 1, 16)))
    for by in (1, 2, 3):
        signal(device(x, on_ring(y, by, 4), z, core))
        signal(device(on_ring(x, by, 4), y, z, core))
    for by in range(4):
        signal(device(on_ring(x, by, 4), y, z, 1 - core))

    @pl.when(holder)
    def _():
        for by in range(1, 16):
            signal(device(x, y, on_ring(z, by, 16), core))

    @pl.when(jnp.logical_not(holder))
    def _():
        signal(device(x, y, carried, core))
        signal(device(x, y, carried + 8, core))

    return lambda: pl.semaphore_wait(barrier, jnp.where(holder, 12 + 15, 12 + 2))


def whole_kernel(
    scale,
    frames_far,
    cotangent_far,
    w_in,
    w_down,
    w_up,
    output,
    input_grad,
    grad_in,
    grad_down,
    grad_up,
    own,
    own_wide,
    frames,
    cotangent,
    frames_above,
    frames_below,
    cotangent_above,
    cotangent_below,
    full,
    parts,
    wide,
    fx,
    h3,
    c3,
    slopes,
    shifted,
    shifted_wide,
    coarse2,
    grad2,
    gx,
    mixed,
    win,
    wdn,
    wup,
    fine,
    down,
    up,
    back_fine,
    back_down,
    back_up,
    *rest,
):
    buffers, rest = rest[:11], rest[11:]
    gather_sems, reduce_sems, (halo_send, halo_recv, load_sem) = rest[:8], rest[8:18], rest[18:]
    band = lax.axis_index("height")
    top, bottom = band == 0, band == lax.axis_size("height") - 1
    under_top, over_bottom = jnp.logical_not(top), jnp.logical_not(bottom)

    loads = [
        pltpu.make_async_copy(frames_far, frames, load_sem.at[0]),
        pltpu.make_async_copy(cotangent_far, cotangent, load_sem.at[1]),
    ]
    every(loads, "start")
    gathers = [Gather(job, own, full, gather_sems) for job in range(3)]
    reduces = [Reduce(job, parts, buffers, reduce_sems, scale) for job in range(3)]

    row = lax.axis_index("dp")
    over, under = (row, on_ring(band, -1, 16)), (row, on_ring(band, 1, 16))

    def halo(slot, source, first, target, where):
        cells = source.at[pl.ds(first, target.shape[0])]
        return remote(cells, target, halo_send.at[slot], halo_recv.at[slot], where)

    downward = [
        halo(0, frames_far, 12, frames_above, under),
        halo(1, cotangent_far, 13, cotangent_above, under),
    ]
    upward = [
        halo(2, frames_far, 0, frames_below, over),
        halo(3, cotangent_far, 0, cotangent_below, over),
    ]

    all_there = greet()
    pack_own(w_in, w_down, w_up, own_wide, own)
    wide[:, 0:8] = jnp.zeros((23, 8, 128), F32)
    wide[:, 136:144] = jnp.zeros((23, 8, 128), F32)
    shifted[:, 0:8] = jnp.zeros((9, 8, 128), F32)
    shifted[:, 72:80] = jnp.zeros((9, 8, 128), F32)
    shifted_wide[:, 64:72] = jnp.zeros((10, 8, 256), F32)
    all_there()
    for job in range(3):
        gathers[job].step(0)

    @pl.when(top)
    def _():
        frames_above[...] = jnp.zeros_like(frames_above)
        cotangent_above[...] = jnp.zeros_like(cotangent_above)

    @pl.when(bottom)
    def _():
        frames_below[...] = jnp.zeros_like(frames_below)
        cotangent_below[...] = jnp.zeros_like(cotangent_below)

    every(loads, "wait")
    gathers[IN].step(1)
    gathers[DOWN].step(1)
    gathers[UP].step(1)
    when(over_bottom, lambda: every(downward, "start"))
    when(under_top, lambda: every(upward, "start"))
    spread_columns(frames, 4, wide, fx, 4)
    gathers[IN].step(2)
    gathers[DOWN].step(2)
    spread_columns(cotangent, 3, wide, c3, 3)
    gathers[IN].step(3)
    gathers[UP].step(2)
    gathers[DOWN].step(3)
    gathers[IN].step(4)
    unpack_in(full, win)
    stack_in(win, fine, back_fine)
    gathers[UP].step(3)
    gathers[DOWN].step(4)
    unpack_down(full, wdn)
    stack_down(wdn, down, back_down)
    gathers[UP].step(4)
    unpack_up(full, wup)
    stack_up(wup, up, back_up)

    when(under_top, lambda: every(downward, "wait_recv"))
    when(over_bottom, lambda: every(upward, "wait_recv"))
    spread_columns(frames_above, 0, wide, fx, 4)
    spread_columns(frames_below, 20, wide, fx, 4)
    spread_columns(cotangent_above, 0, wide, c3, 3)
    spread_columns(cotangent_below, 19, wide, c3, 3)

    for first in (0, 7, 14):
        pre = sum(matmul(flat(fx[first + j : first + j + 7]), fine[j]) for j in range(3))
        gate = sigmoid(pre)
        hidden = (pre * gate).reshape(7, 64, 256)
        slope = (gate * (1.0 + pre * (1.0 - gate))).reshape(7, 64, 256)
        shifted[0:7, 8:72] = hidden[:, :, 128:256]
        before = shifted[0:7, 7:71].astype(BF16)
        hidden = hidden.astype(BF16)
        for row in range(7):
            i = first + row
            h3[i // 2, i % 2, :, 0:128] = before[row]
            h3[i // 2, i % 2, :, 128:384] = hidden[row]
            if 2 <= i < 20:
                slopes[i - 2] = slope[row]

    @pl.when(top)
    def _():
        for i in range(3):
            h3[i // 2, i % 2] = jnp.zeros((64, 384), BF16)

    @pl.when(bottom)
    def _():
        for i in (19, 20):
            h3[i // 2, i % 2] = jnp.zeros((64, 384), BF16)

    views = ((0, 0), (0, 1), (1, 0))
    pre = sum(matmul(flat(h3[a : a + 10, b]), down[j]) for j, (a, b) in enumerate(views))
    gate = sigmoid(pre)
    coarse = (pre * gate).reshape(10, 64, 256)
    shifted_wide[:, 0:64] = coarse
    coarse2[:, :, 0:256] = coarse.astype(BF16)
    coarse2[:, :, 256:512] = shifted_wide[:, 1:65].astype(BF16)
    back = sum(matmul_t(flat(c3[a : a + 10, b]), back_up[j]) for j, (a, b) in enumerate(views))
    grad = (back * (gate * (1.0 + pre * (1.0 - gate)))).reshape(10, 64, 256)
    shifted_wide[:, 0:64] = grad
    grad2[:, :, 0:256] = grad.astype(BF16)
    grad2[:, :, 256:512] = shifted_wide[:, 1:65].astype(BF16)

    @pl.when(top)
    def _():
        grad2[0] = jnp.zeros((64, 512), BF16)

    @pl.when(bottom)
    def _():
        coarse2[9] = jnp.zeros((64, 512), BF16)
        grad2[9] = jnp.zeros((64, 512), BF16)

    turned = flat(coarse2[1:9, :, 0:256]).T
    for j, (a, b) in enumerate(views):
        found = matmul(turned, flat(c3[a + 1 : a + 9, b]))
        for slot in range(3):
            wup[3 * (2 - j) + 2 - slot] = found[:, slot * 128 : slot * 128 + 128].astype(BF16)
    pack_up(parts, wup)
    reduces[UP].step(0)
    turned = flat(grad2[1:9, :, 0:256]).T
    for j, (a, b) in enumerate(views):
        found = matmul(turned, flat(h3[a + 1 : a + 9, b]))
        for slot in range(3):
            wdn[3 * j + slot] = found[:, slot * 128 : slot * 128 + 128].T.astype(BF16)
    pack_down(parts, wdn)
    reduces[DOWN].step(0)
    reduces[UP].step(1)

    grad_even = matmul_t(flat(grad2[1:10]), back_down[1]).reshape(9, 64, 256)
    grad_odd = (
        matmul_t(flat(grad2[0:9]), back_down[2]) + matmul_t(flat(grad2[1:10]), back_down[0])
    ).reshape(9, 64, 256)
    for start, rows in ((0, grad_odd), (1, grad_even)):
        rows = jnp.concatenate([rows[m : m + 1] * slopes[start + 2 * m][None] for m in range(9)], axis=0)
        ready = rows.astype(BF16)
        shifted[:, 8:72] = rows[:, :, 128:256]
        before = shifted[:, 7:71].astype(BF16)
        shifted[:, 8:72] = rows[:, :, 0:128]
        after = shifted[:, 9:73].astype(BF16)
        for m in range(9):
            gx[start + 2 * m, :, 0:128] = before[m]
            gx[start + 2 * m, :, 128:384] = ready[m]
            gx[start + 2 * m, :, 384:512] = after[m]

    @pl.when(top)
    def _():
        gx[0] = jnp.zeros((64, 512), BF16)

    @pl.when(bottom)
    def _():
        gx[17] = jnp.zeros((64, 512), BF16)

    reduces[DOWN].step(1)
    turned = flat(gx[1:17, :, 128:384]).T
    for j in range(3):
        found = matmul(turned, flat(fx[3 + j : 19 + j]))
        for l in range(3):
            both = found[0:128, l * 128 : l * 128 + 128] + found[128:256, (l + 1) * 128 : (l + 2) * 128]
            win[3 * j + l] = both.T.astype(BF16)
    pack_in(parts, win)
    reduces[IN].step(0)
    reduces[UP].step(2)
    reduces[IN].step(1)

    def mix(row, cells):
        mixed[row, pl.ds(0, 64, stride=2), :] = cells[:, 0:128]
        mixed[row, pl.ds(1, 64, stride=2), :] = cells[:, 128:256]

    even = matmul(flat(coarse2[1:9]), up[1])
    odd = matmul(flat(coarse2[1:9]), up[0]) + matmul(flat(coarse2[2:10]), up[2])
    for t in range(8):
        mix(2 * t, even[64 * t : 64 * t + 64])
        mix(2 * t + 1, odd[64 * t : 64 * t + 64])
    output[...] = (frames[...].astype(F32) + mixed[...]).astype(BF16)
    reduces[DOWN].step(2)
    reduces[UP].step(3)
    reduces[IN].step(2)

    for first in (0, 8):
        back = sum(matmul_t(flat(gx[first + j : first + j + 8]), back_fine[j]) for j in range(3))
        for row in range(8):
            mix(first + row, back[64 * row : 64 * row + 64])
    input_grad[...] = (cotangent[...].astype(F32) + mixed[...]).astype(BF16)
    reduces[DOWN].step(3)
    reduces[IN].step(3)
    for job in (UP, DOWN, IN):
        reduces[job].step(4)
    for job in (UP, DOWN, IN):
        reduces[job].step(5)

    take_share(buffers[10], band, grad_in, grad_down, grad_up)
    for job in range(3):
        gathers[job].step(5)
        reduces[job].step(6)
    when(over_bottom, lambda: every(downward, "wait_send"))
    when(under_top, lambda: every(upward, "wait_send"))


def whole(frames, cotangent, w_in, w_down, w_up, scale):
    vmem, dma = pltpu.VMEM, pltpu.SemaphoreType.DMA
    spec, far = pl.BlockSpec(memory_space=vmem), pl.BlockSpec(memory_space=pl.ANY)
    gather_counts = (7, 1, 4, 4, 4, 4, 4, 4)
    reduce_counts = (4, 4, 4, 4, 4, 4, 2, 15, 8, 1)
    return pl.pallas_call(
        functools.partial(whole_kernel, scale),
        out_shape=(
            jax.ShapeDtypeStruct((16, 128, 128), BF16),
            jax.ShapeDtypeStruct((16, 128, 128), BF16),
            jax.ShapeDtypeStruct((3, 3, 4, 8), F32),
            jax.ShapeDtypeStruct((3, 3, 4, 16), F32),
            jax.ShapeDtypeStruct((3, 3, 8, 8), F32),
        ),
        in_specs=[far, far, spec, spec, spec],
        out_specs=(spec,) * 5,
        scratch_shapes=[
            vmem((PACK, 128), BF16),
            vmem((PACK, 128), F32),
            vmem((16, 128, 128), BF16),
            vmem((16, 128, 128), BF16),
            vmem((4, 128, 128), BF16),
            vmem((3, 128, 128), BF16),
            vmem((3, 128, 128), BF16),
            vmem((2, 128, 128), BF16),
            vmem((8, 4, PACK, 128), BF16),
            vmem((8, 4, PACK, 128), BF16),
            vmem((23, 144, 128), F32),
            vmem((23, 64, 512), BF16),
            vmem((11, 2, 64, 384), BF16),
            vmem((11, 2, 64, 384), BF16),
            vmem((18, 64, 256), F32),
            vmem((9, 80, 128), F32),
            vmem((10, 72, 256), F32),
            vmem((10, 64, 512), BF16),
            vmem((10, 64, 512), BF16),
            vmem((18, 64, 512), BF16),
            vmem((16, 128, 128), F32),
            vmem((9, 128, 128), BF16),
            vmem((9, 128, 256), BF16),
            vmem((9, 256, 128), BF16),
            vmem((3, 512, 256), BF16),
            vmem((3, 384, 256), BF16),
            vmem((3, 512, 256), BF16),
            vmem((3, 256, 512), BF16),
            vmem((3, 256, 512), BF16),
            vmem((3, 256, 384), BF16),
            vmem((4, 4, PACK, 128), BF16),
            vmem((3, 4, PACK, 128), BF16),
            vmem((3, 4, PACK, 128), BF16),
            vmem((4, PACK, 128), F32),
            vmem((3, PACK, 128), BF16),
            vmem((3, PACK, 128), BF16),
            vmem((PACK, 128), F32),
            vmem((PACK, 128), BF16),
            vmem((15, PACK, 128), BF16),
            vmem((PACK, 128), F32),
            vmem((PACK, 128), F32),
        ]
        + [dma((3, count)) for count in gather_counts + reduce_counts]
        + [dma((4,)), dma((4,)), dma((2,))],
        compiler_params=pltpu.CompilerParams(
            collective_id=0, has_side_effects=True, vmem_limit_bytes=56 << 20
        ),
    )(frames, cotangent, w_in, w_down, w_up)


def on_device(frames, cotangent, w_in, w_down, w_up):
    frames, cotangent = frames[0], cotangent[0]
    pixel_count = lax.axis_size("dp") * lax.axis_size("height") * frames.shape[0] * frames.shape[1]
    output, input_grad, *grads = whole(frames, cotangent, w_in, w_down, w_up, 1.0 / math.sqrt(pixel_count))
    return (output[None], input_grad[None], *grads)


def solution(mesh):
    in_specs = (
        P("dp", "height", None, None),
        P("dp", "height", None, None),
        P(None, None, "dp", None),
        P(None, None, "dp", None),
        P(None, None, "dp", None),
    )
    out_specs = (
        P("dp", "height", None, None),
        P("dp", "height", None, None),
        P(None, None, "dp", "height"),
        P(None, None, "dp", "height"),
        P(None, None, "dp", "height"),
    )
    return jax.shard_map(
        on_device, mesh=mesh, in_specs=in_specs, out_specs=out_specs, check_vma=False
    )
```

time: 1400 us -> 86.7 us (0.06)
  waiting for transfers between devices: 706 us -> 0 us
  blocking collectives: 464 us -> 0 us
  starting transfers between devices: 112 us -> 0 us
  Pallas kernels: 0 us -> 80.4 us
  local copies, waits for them, and re-layouts: 61.1 us -> 4.58 us
  matrix products: 24.9 us -> 0 us
  between operations: 16.2 us -> 0.65 us
    unnamed x5 -> x0, waiting for transfers between devices: 478 us -> none
    all_gather x3 -> x0, blocking collectives: 328 us -> none  [the longest x1 116 us: on_device(): full_up = lax.all_gather(w_up, 'dp', axis=2, tiled=True)]
    reduce_scatter x1 -> x0, waiting for transfers between devices: 212 us -> none  [on_device(): lax.psum_scatter(grad_third, 'dp', scatter_dimension=2, tiled=True)]
    unnamed x1 -> x0, blocking collectives: 136 us -> none
    ppermute x8 -> x0, starting transfers between devices: 112 us -> none  [the longest x4 78.7 us: from_behind(): return lax.ppermute(shard, axis, pairs)]
    pallas_call x0 -> x1, Pallas kernels: none -> 80.4 us  [whole(): pl.pallas_call(functools.partial(whole_kernel, scale), out_shape=(jax.Sha...]
    slice x20 -> x0, local copies, waits for them, and re-layouts: 29.5 us -> none  [the longest x18 28.8 us: kernel_grad(): source[:, row_tap:row_tap + stride * (rows_out - 1) + 1:stride, col_tap:c...]
    ppermute x8 -> x0, waiting for transfers between devices: 15.9 us -> none  [the longest x4 15.9 us: from_behind(): return lax.ppermute(shard, axis, pairs)]
  transfers between devices with their start and end apart: 11 -> 0, of which waited for: 5 -> 0; matrix products, arithmetic and copies ran while one was open for 4% -> 0% of each run, Pallas kernels for 0% -> 0%
where the time goes in v1:
time: 86.7 us; the launch traced here: 85.6 us
  Pallas kernels  80.4 us (93%)
  local copies, waits for them, and re-layouts  4.58 us (5%)
    pallas_call x1, Pallas kernels, whole(): pl.pallas_call(functools.partial(whole_kernel, scale), out_shape=(jax.Sha...  80.4 us
    unnamed x13, local copies, waits for them, and re-layouts  4.58 us

profile of v1, /device:TPU:1, one launch (start us, length us, event | category | flops | bytes accessed | tf_op | source)
XLA Modules:
  0.0 85.6 jit_solution(8327125355340066966)
XLA Ops:
  0.6 80.4 %shard_map.92 = (bf16[16,128,128]{2,1,0:T(8,128)(2,1)}, bf16[16,128,128]{2,1,0:T(8,128)(2,1)}, f32[3,3,4,8]{3,2,1,0:T(4,128)}, f32[3,3,4,16]{3,2,1,0:T(4,128)}, f32[3,3,8,8]{3,2,1,0:T(8,128)}) custom-call(bf16[16,128,128]{2,1,0:T(8,128)(2,1)} %bitcast.4, bf16[16,128,128]{2,1,0:T(8,128)(2,1)} %bitcast.5, bf16[3,3,4,128]{3,2,1,0:T(4,128)(2,1)} %w_in.1, ...), custom_call_target="tpu_custom_call" | custom-call | tf_op jit(solution)/shard_map/pallas_call | solution.py:706
  81.0 0.0 copy-start
  81.0 1.9 %copy.15 = bf16[1,16,128,128]{3,2,1,0:T(8,128)(2,1)} copy(bf16[1,16,128,128]{3,2,1,0:T(8,128)(2,1)} %bitcast.7) | data formatting | bytes 1048576
  82.9 0.0 copy-done
  82.9 0.0 copy-start.3
  82.9 0.0 copy-start.2
  83.0 0.8 copy.16
  83.7 0.0 copy-done.3
  83.7 0.0 copy-start.1
  83.7 0.6 copy.17
  84.4 0.0 copy-done.2
  84.4 0.6 copy.18
  85.0 0.0 copy-done.1
  85.0 0.6 copy.19
Async XLA Ops:
  81.0 2.0 %copy-start = (bf16[16,128,128]{2,1,0:T(8,128)(2,1)S(1)}, bf16[16,128,128]{2,1,0:T(8,128)(2,1)}, u32[]{:S(2)}) copy-start(bf16[16,128,128]{2,1,0:T(8,128)(2,1)} %get-tuple-element.11) | copy-start | bytes 1572868
  82.9 0.8 copy-start.3
  82.9 1.4 %copy-start.2 = (f32[3,3,4,16]{3,2,1,0:T(4,128)S(1)}, f32[3,3,4,16]{3,2,1,0:T(4,128)}, u32[]{:S(2)}) copy-start(f32[3,3,4,16]{3,2,1,0:T(4,128)} %get-tuple-element.23) | copy-start | bytes 6916
  83.7 1.2 %copy-start.1 = (f32[3,3,8,8]{3,2,1,0:T(8,128)S(1)}, f32[3,3,8,8]{3,2,1,0:T(8,128)}, u32[]{:S(2)}) copy-start(f32[3,3,8,8]{3,2,1,0:T(8,128)} %get-tuple-element.24) | copy-start | bytes 6916

commit v2 on v1

--- a/solution.py
+++ b/solution.py
@@ -287,10 +287,11 @@
         self.parts = parts
         (
             self.from_core, self.heavy_out, self.heavy_in, self.sums, self.light_out, self.light_in,
-            self.column, self.z_out, self.z_in, self.done, self.total,
+            self.column, self.z_out, self.z_in, self.done, self.total, self.direct_out, self.direct_in,
         ) = buffers
         self.sems = [sem.at[job] for sem in sems]
         self.scale = scale
+        self.at_once = job == IN
         self.x, self.y, self.z, self.core = place()
         self.carried = self.x + 4 * self.core
         self.holder = lax.rem(self.z, 8) == self.carried
@@ -321,6 +322,37 @@
             self.light_out.at[by - 1, self.rows], self.light_in.at[by - 1, self.rows],
             self.sems[4].at[by], self.sems[5].at[by], self.beside(axis, by),
         )
+
+    def direct(self, slot):
+        where = device(on_ring(self.x, slot // 4, 4), on_ring(self.y, slot % 4, 4), self.z, self.core)
+        return remote(
+            self.direct_out.at[slot], self.direct_in.at[slot], self.sems[10].at[slot], self.sems[11].at[slot], where
+        )
+
+    def step_direct(self, stage):
+        rows = self.rows
+        if stage == 1:
+            for by in (2, 1, 3, 0):
+                self.across(by).wait_recv()
+                self.sums[:, rows] = self.both(by)
+                for turn in (2, 1, 3, 0):
+                    if by or turn:
+                        slot = 4 * by + turn
+                        self.direct_out[slot] = self.sums[on_ring(self.y, turn, 4), rows].astype(BF16)
+                        self.direct(slot).start()
+            self.column[rows] = self.sums[self.y, rows]
+        if stage == 3:
+            total = self.column[rows]
+            for slot in (4, 12, 1, 3, 8, 2, 5, 7, 13, 15, 6, 9, 11, 14, 10):
+                self.direct(slot).wait_recv()
+                total += self.direct_in[slot].astype(F32)
+            self.column[rows] = total
+            self.send_to_holders(total)
+
+    def send_to_holders(self, total):
+        self.z_out[self.rows] = total.astype(BF16)
+        for at in (0, 8):
+            when(self.z != self.carried + at, self.to_holder(at).start)
 
     def to_holder(self, at):
         where = self.carried + at
@@ -352,6 +384,8 @@
 
     def step(self, stage):
         rows = self.rows
+        if self.at_once and stage in (1, 2, 3):
+            return self.step_direct(stage)
         if stage == 0:
             for by in (1, 3, 2, 0):
                 self.across(by).start()
@@ -379,9 +413,7 @@
                 self.light(by).wait_recv()
                 total += self.light_in[by - 1, rows].astype(F32)
             self.column[rows] = total
-            self.z_out[rows] = total.astype(BF16)
-            for at in (0, 8):
-                when(self.z != self.carried + at, self.to_holder(at).start)
+            self.send_to_holders(total)
         if stage == 4:
 
             @pl.when(self.holder)
@@ -400,9 +432,13 @@
         if stage == 6:
             for by in range(4):
                 self.across(by).wait_send()
-            for by in (1, 2, 3):
-                self.heavy(by).wait_send()
-                self.light(by).wait_send()
+            if self.at_once:
+                for slot in range(1, 16):
+                    self.direct(slot).wait_send()
+            else:
+                for by in (1, 2, 3):
+                    self.heavy(by).wait_send()
+                    self.light(by).wait_send()
             for at in (0, 8):
                 when(self.z != self.carried + at, self.to_holder(at).wait_send)
             when(self.holder, lambda: every(self.spread(), "wait_send"))
@@ -420,15 +456,10 @@
 
     signal((row, on_ring(band, -1, 16)))
     signal((row, on_ring(band, 1, 16)))
-    for by in (1, 2, 3):
-        signal(device(x, on_ring(y, by, 4), z, core))
-        signal(device(on_ring(x, by, 4), y, z, core))
-    for by in range(4):
-        signal(device(on_ring(x, by, 4), y, z, 1 - core))
 
     @pl.when(holder)
     def _():
-        for by in range(1, 16):
+        for by in (8, 7, 9, 6, 10, 5, 11, 4, 12, 3, 13, 2, 14, 1, 15):
             signal(device(x, y, on_ring(z, by, 16), core))
 
     @pl.when(jnp.logical_not(holder))
@@ -436,7 +467,11 @@
         signal(device(x, y, carried, core))
         signal(device(x, y, carried + 8, core))
 
-    return lambda: pl.semaphore_wait(barrier, jnp.where(holder, 12 + 15, 12 + 2))
+    for slot in (10, 6, 14, 9, 11, 5, 7, 13, 15, 8, 2, 4, 12, 1, 3):
+        signal(device(on_ring(x, slot // 4, 4), on_ring(y, slot % 4, 4), z, core))
+    for by in (2, 1, 3, 0):
+        signal(device(on_ring(x, by, 4), y, z, 1 - core))
+    return lambda: pl.semaphore_wait(barrier, jnp.where(holder, 21 + 15, 21 + 2))
 
 
 def whole_kernel(
@@ -459,6 +494,8 @@
     frames_below,
     cotangent_above,
     cotangent_below,
+    grad_above,
+    grad_below,
     full,
     parts,
     wide,
@@ -483,8 +520,8 @@
     back_up,
     *rest,
 ):
-    buffers, rest = rest[:11], rest[11:]
-    gather_sems, reduce_sems, (halo_send, halo_recv, load_sem) = rest[:8], rest[8:18], rest[18:]
+    buffers, rest = rest[:13], rest[13:]
+    gather_sems, reduce_sems, (halo_send, halo_recv, load_sem) = rest[:8], rest[8:20], rest[20:]
     band = lax.axis_index("height")
     top, bottom = band == 0, band == lax.axis_size("height") - 1
     under_top, over_bottom = jnp.logical_not(top), jnp.logical_not(bottom)
@@ -505,8 +542,8 @@
         return remote(cells, target, halo_send.at[slot], halo_recv.at[slot], where)
 
     downward = [
-        halo(0, frames_far, 12, frames_above, under),
-        halo(1, cotangent_far, 13, cotangent_above, under),
+        halo(0, frames_far, 14, frames_above, under),
+        halo(1, cotangent_far, 15, cotangent_above, under),
     ]
     upward = [
         halo(2, frames_far, 0, frames_below, over),
@@ -519,7 +556,9 @@
     wide[:, 136:144] = jnp.zeros((23, 8, 128), F32)
     shifted[:, 0:8] = jnp.zeros((9, 8, 128), F32)
     shifted[:, 72:80] = jnp.zeros((9, 8, 128), F32)
-    shifted_wide[:, 64:72] = jnp.zeros((10, 8, 256), F32)
+    shifted_wide[:, 64:72] = jnp.zeros((9, 8, 256), F32)
+    every(loads, "wait")
+    spread_columns(frames, 4, wide, fx, 4)
     all_there()
     for job in range(3):
         gathers[job].step(0)
@@ -534,13 +573,11 @@
         frames_below[...] = jnp.zeros_like(frames_below)
         cotangent_below[...] = jnp.zeros_like(cotangent_below)
 
-    every(loads, "wait")
     gathers[IN].step(1)
     gathers[DOWN].step(1)
     gathers[UP].step(1)
     when(over_bottom, lambda: every(downward, "start"))
     when(under_top, lambda: every(upward, "start"))
-    spread_columns(frames, 4, wide, fx, 4)
     gathers[IN].step(2)
     gathers[DOWN].step(2)
     spread_columns(cotangent, 3, wide, c3, 3)
@@ -560,97 +597,94 @@
 
     when(under_top, lambda: every(downward, "wait_recv"))
     when(over_bottom, lambda: every(upward, "wait_recv"))
-    spread_columns(frames_above, 0, wide, fx, 4)
+    spread_columns(frames_above, 2, wide, fx, 4)
     spread_columns(frames_below, 20, wide, fx, 4)
-    spread_columns(cotangent_above, 0, wide, c3, 3)
+    spread_columns(cotangent_above, 2, wide, c3, 3)
     spread_columns(cotangent_below, 19, wide, c3, 3)
 
-    for first in (0, 7, 14):
-        pre = sum(matmul(flat(fx[first + j : first + j + 7]), fine[j]) for j in range(3))
+    for first, count in ((2, 7), (9, 6), (15, 6)):
+        pre = sum(matmul(flat(fx[first + j : first + j + count]), fine[j]) for j in range(3))
         gate = sigmoid(pre)
-        hidden = (pre * gate).reshape(7, 64, 256)
-        slope = (gate * (1.0 + pre * (1.0 - gate))).reshape(7, 64, 256)
-        shifted[0:7, 8:72] = hidden[:, :, 128:256]
-        before = shifted[0:7, 7:71].astype(BF16)
+        hidden = (pre * gate).reshape(count, 64, 256)
+        slope = (gate * (1.0 + pre * (1.0 - gate))).reshape(count, 64, 256)
+        shifted[0:count, 8:72] = hidden[:, :, 128:256]
+        before = shifted[0:count, 7:71].astype(BF16)
         hidden = hidden.astype(BF16)
-        for row in range(7):
+        for row in range(count):
             i = first + row
             h3[i // 2, i % 2, :, 0:128] = before[row]
             h3[i // 2, i % 2, :, 128:384] = hidden[row]
-            if 2 <= i < 20:
-                slopes[i - 2] = slope[row]
+            if 3 <= i < 19:
+                slopes[i - 3] = slope[row]
 
     @pl.when(top)
     def _():
-        for i in range(3):
-            h3[i // 2, i % 2] = jnp.zeros((64, 384), BF16)
+        h3[1, 0] = jnp.zeros((64, 384), BF16)
 
     @pl.when(bottom)
     def _():
         for i in (19, 20):
             h3[i // 2, i % 2] = jnp.zeros((64, 384), BF16)
 
-    views = ((0, 0), (0, 1), (1, 0))
-    pre = sum(matmul(flat(h3[a : a + 10, b]), down[j]) for j, (a, b) in enumerate(views))
+    views = ((1, 0), (1, 1), (2, 0))
+    pre = sum(matmul(flat(h3[a : a + 9, b]), down[j]) for j, (a, b) in enumerate(views))
     gate = sigmoid(pre)
-    coarse = (pre * gate).reshape(10, 64, 256)
+    coarse = (pre * gate).reshape(9, 64, 256)
     shifted_wide[:, 0:64] = coarse
     coarse2[:, :, 0:256] = coarse.astype(BF16)
     coarse2[:, :, 256:512] = shifted_wide[:, 1:65].astype(BF16)
-    back = sum(matmul_t(flat(c3[a : a + 10, b]), back_up[j]) for j, (a, b) in enumerate(views))
-    grad = (back * (gate * (1.0 + pre * (1.0 - gate)))).reshape(10, 64, 256)
+    back = sum(matmul_t(flat(c3[a : a + 9, b]), back_up[j]) for j, (a, b) in enumerate(views))
+    grad = (back * (gate * (1.0 + pre * (1.0 - gate)))).reshape(9, 64, 256)
     shifted_wide[:, 0:64] = grad
     grad2[:, :, 0:256] = grad.astype(BF16)
     grad2[:, :, 256:512] = shifted_wide[:, 1:65].astype(BF16)
 
-    @pl.when(top)
-    def _():
-        grad2[0] = jnp.zeros((64, 512), BF16)
-
     @pl.when(bottom)
     def _():
-        coarse2[9] = jnp.zeros((64, 512), BF16)
-        grad2[9] = jnp.zeros((64, 512), BF16)
-
-    turned = flat(coarse2[1:9, :, 0:256]).T
+        coarse2[8] = jnp.zeros((64, 512), BF16)
+        grad2[8] = jnp.zeros((64, 512), BF16)
+
+    turned = flat(coarse2[0:8, :, 0:256]).T
     for j, (a, b) in enumerate(views):
-        found = matmul(turned, flat(c3[a + 1 : a + 9, b]))
+        found = matmul(turned, flat(c3[a : a + 8, b]))
         for slot in range(3):
             wup[3 * (2 - j) + 2 - slot] = found[:, slot * 128 : slot * 128 + 128].astype(BF16)
     pack_up(parts, wup)
     reduces[UP].step(0)
-    turned = flat(grad2[1:9, :, 0:256]).T
+    turned = flat(grad2[0:8, :, 0:256]).T
     for j, (a, b) in enumerate(views):
-        found = matmul(turned, flat(h3[a + 1 : a + 9, b]))
+        found = matmul(turned, flat(h3[a : a + 8, b]))
         for slot in range(3):
             wdn[3 * j + slot] = found[:, slot * 128 : slot * 128 + 128].T.astype(BF16)
     pack_down(parts, wdn)
     reduces[DOWN].step(0)
     reduces[UP].step(1)
 
-    grad_even = matmul_t(flat(grad2[1:10]), back_down[1]).reshape(9, 64, 256)
+    grad_even = matmul_t(flat(grad2[0:8]), back_down[1]).reshape(8, 64, 256)
     grad_odd = (
-        matmul_t(flat(grad2[0:9]), back_down[2]) + matmul_t(flat(grad2[1:10]), back_down[0])
-    ).reshape(9, 64, 256)
-    for start, rows in ((0, grad_odd), (1, grad_even)):
-        rows = jnp.concatenate([rows[m : m + 1] * slopes[start + 2 * m][None] for m in range(9)], axis=0)
+        matmul_t(flat(grad2[0:8]), back_down[2]) + matmul_t(flat(grad2[1:9]), back_down[0])
+    ).reshape(8, 64, 256)
+
+    def store_grad(rows, places):
+        count = len(places)
         ready = rows.astype(BF16)
-        shifted[:, 8:72] = rows[:, :, 128:256]
-        before = shifted[:, 7:71].astype(BF16)
-        shifted[:, 8:72] = rows[:, :, 0:128]
-        after = shifted[:, 9:73].astype(BF16)
-        for m in range(9):
-            gx[start + 2 * m, :, 0:128] = before[m]
-            gx[start + 2 * m, :, 128:384] = ready[m]
-            gx[start + 2 * m, :, 384:512] = after[m]
-
-    @pl.when(top)
-    def _():
-        gx[0] = jnp.zeros((64, 512), BF16)
-
-    @pl.when(bottom)
-    def _():
-        gx[17] = jnp.zeros((64, 512), BF16)
+        shifted[0:count, 8:72] = rows[:, :, 128:256]
+        before = shifted[0:count, 7:71].astype(BF16)
+        shifted[0:count, 8:72] = rows[:, :, 0:128]
+        after = shifted[0:count, 9:73].astype(BF16)
+        for m, k in enumerate(places):
+            gx[k, :, 0:128] = before[m]
+            gx[k, :, 128:384] = ready[m]
+            gx[k, :, 384:512] = after[m]
+
+    for start, rows in ((1, grad_even), (2, grad_odd)):
+        places = range(start, start + 16, 2)
+        rows = jnp.concatenate([rows[m : m + 1] * slopes[k - 1][None] for m, k in enumerate(places)], axis=0)
+        store_grad(rows, places)
+    grad_down_copy = [remote(gx.at[16, :, 128:384], grad_above, halo_send.at[4], halo_recv.at[4], under)]
+    grad_up_copy = [remote(gx.at[1, :, 128:384], grad_below, halo_send.at[5], halo_recv.at[5], over)]
+    when(over_bottom, lambda: every(grad_down_copy, "start"))
+    when(under_top, lambda: every(grad_up_copy, "start"))
 
     reduces[DOWN].step(1)
     turned = flat(gx[1:17, :, 128:384]).T
@@ -668,8 +702,8 @@
         mixed[row, pl.ds(0, 64, stride=2), :] = cells[:, 0:128]
         mixed[row, pl.ds(1, 64, stride=2), :] = cells[:, 128:256]
 
-    even = matmul(flat(coarse2[1:9]), up[1])
-    odd = matmul(flat(coarse2[1:9]), up[0]) + matmul(flat(coarse2[2:10]), up[2])
+    even = matmul(flat(coarse2[0:8]), up[1])
+    odd = matmul(flat(coarse2[0:8]), up[0]) + matmul(flat(coarse2[1:9]), up[2])
     for t in range(8):
         mix(2 * t, even[64 * t : 64 * t + 64])
         mix(2 * t + 1, odd[64 * t : 64 * t + 64])
@@ -678,13 +712,26 @@
     reduces[UP].step(3)
     reduces[IN].step(2)
 
+    reduces[DOWN].step(3)
+    reduces[IN].step(3)
+
+    @pl.when(top)
+    def _():
+        grad_above[...] = jnp.zeros_like(grad_above)
+
+    @pl.when(bottom)
+    def _():
+        grad_below[...] = jnp.zeros_like(grad_below)
+
+    when(under_top, lambda: every(grad_down_copy, "wait_recv"))
+    when(over_bottom, lambda: every(grad_up_copy, "wait_recv"))
+    store_grad(grad_above[...].astype(F32)[None], (0,))
+    store_grad(grad_below[...].astype(F32)[None], (17,))
     for first in (0, 8):
         back = sum(matmul_t(flat(gx[first + j : first + j + 8]), back_fine[j]) for j in range(3))
         for row in range(8):
             mix(first + row, back[64 * row : 64 * row + 64])
     input_grad[...] = (cotangent[...].astype(F32) + mixed[...]).astype(BF16)
-    reduces[DOWN].step(3)
-    reduces[IN].step(3)
     for job in (UP, DOWN, IN):
         reduces[job].step(4)
     for job in (UP, DOWN, IN):
@@ -696,13 +743,15 @@
         reduces[job].step(6)
     when(over_bottom, lambda: every(downward, "wait_send"))
     when(under_top, lambda: every(upward, "wait_send"))
+    when(over_bottom, lambda: every(grad_down_copy, "wait_send"))
+    when(under_top, lambda: every(grad_up_copy, "wait_send"))
 
 
 def whole(frames, cotangent, w_in, w_down, w_up, scale):
     vmem, dma = pltpu.VMEM, pltpu.SemaphoreType.DMA
     spec, far = pl.BlockSpec(memory_space=vmem), pl.BlockSpec(memory_space=pl.ANY)
     gather_counts = (7, 1, 4, 4, 4, 4, 4, 4)
-    reduce_counts = (4, 4, 4, 4, 4, 4, 2, 15, 8, 1)
+    reduce_counts = (4, 4, 4, 4, 4, 4, 2, 15, 8, 1, 16, 16)
     return pl.pallas_call(
         functools.partial(whole_kernel, scale),
         out_shape=(
@@ -719,21 +768,23 @@
             vmem((PACK, 128), F32),
             vmem((16, 128, 128), BF16),
             vmem((16, 128, 128), BF16),
-            vmem((4, 128, 128), BF16),
+            vmem((2, 128, 128), BF16),
             vmem((3, 128, 128), BF16),
-            vmem((3, 128, 128), BF16),
+            vmem((1, 128, 128), BF16),
             vmem((2, 128, 128), BF16),
+            vmem((64, 256), BF16),
+            vmem((64, 256), BF16),
             vmem((8, 4, PACK, 128), BF16),
             vmem((8, 4, PACK, 128), BF16),
             vmem((23, 144, 128), F32),
             vmem((23, 64, 512), BF16),
             vmem((11, 2, 64, 384), BF16),
             vmem((11, 2, 64, 384), BF16),
-            vmem((18, 64, 256), F32),
+            vmem((16, 64, 256), F32),
             vmem((9, 80, 128), F32),
-            vmem((10, 72, 256), F32),
-            vmem((10, 64, 512), BF16),
-            vmem((10, 64, 512), BF16),
+            vmem((9, 72, 256), F32),
+            vmem((9, 64, 512), BF16),
+            vmem((9, 64, 512), BF16),
             vmem((18, 64, 512), BF16),
             vmem((16, 128, 128), F32),
             vmem((9, 128, 128), BF16),
@@ -756,19 +807,38 @@
             vmem((15, PACK, 128), BF16),
             vmem((PACK, 128), F32),
             vmem((PACK, 128), F32),
+            vmem((16, DOWN_AT, 128), BF16),
+            vmem((16, DOWN_AT, 128), BF16),
         ]
         + [dma((3, count)) for count in gather_counts + reduce_counts]
-        + [dma((4,)), dma((4,)), dma((2,))],
+        + [dma((6,)), dma((6,)), dma((2,))],
         compiler_params=pltpu.CompilerParams(
             collective_id=0, has_side_effects=True, vmem_limit_bytes=56 << 20
         ),
     )(frames, cotangent, w_in, w_down, w_up)
 
 
+def hand_on_kernel(*refs):
+    half = len(refs) // 2
+    for source, target in zip(refs[:half], refs[half:]):
+        target[...] = source[...]
+
+
+def hand_on(arrays):
+    spec = pl.BlockSpec(memory_space=pltpu.VMEM)
+    return pl.pallas_call(
+        hand_on_kernel,
+        out_shape=tuple(jax.ShapeDtypeStruct(array.shape, array.dtype) for array in arrays),
+        in_specs=[spec] * len(arrays),
+        out_specs=(spec,) * len(arrays),
+        compiler_params=pltpu.CompilerParams(vmem_limit_bytes=56 << 20),
+    )(*arrays)
+
+
 def on_device(frames, cotangent, w_in, w_down, w_up):
     frames, cotangent = frames[0], cotangent[0]
     pixel_count = lax.axis_size("dp") * lax.axis_size("height") * frames.shape[0] * frames.shape[1]
-    output, input_grad, *grads = whole(frames, cotangent, w_in, w_down, w_up, 1.0 / math.sqrt(pixel_count))
+    output, input_grad, *grads = hand_on(whole(frames, cotangent, w_in, w_down, w_up, 1.0 / math.sqrt(pixel_count)))
     return (output[None], input_grad[None], *grads)
 
 

time: 86.7 us -> 78.1 us (0.901)
  the two profiles are of different devices: /device:TPU:1 before, /device:TPU:3 now
where the time goes in v2:
time: 78.1 us; the launch traced here: 77.8 us
  Pallas kernels  77.2 us (99%)
    pallas_call x1, Pallas kernels, whole(): pl.pallas_call(functools.partial(whole_kernel, scale), out_shape=(jax.Sha...  75 us
    pallas_call x1, Pallas kernels, hand_on(): pl.pallas_call(hand_on_kernel, out_shape=tuple((jax.ShapeDtypeStruct(arra...  2.24 us

profile of v2, /device:TPU:3, one launch (start us, length us, event | category | flops | bytes accessed | tf_op | source)
XLA Modules:
  0.0 77.8 jit_solution(9469232661539113997)
XLA Ops:
  0.6 75.0 %shard_map.92 = (bf16[16,128,128]{2,1,0:T(8,128)(2,1)}, bf16[16,128,128]{2,1,0:T(8,128)(2,1)}, f32[3,3,4,8]{3,2,1,0:T(4,128)}, f32[3,3,4,16]{3,2,1,0:T(4,128)}, f32[3,3,8,8]{3,2,1,0:T(8,128)}) custom-call(bf16[16,128,128]{2,1,0:T(8,128)(2,1)} %bitcast.4, bf16[16,128,128]{2,1,0:T(8,128)(2,1)} %bitcast.5, bf16[3,3,4,128]{3,2,1,0:T(4,128)(2,1)} %w_in.1, ...), custom_call_target="tpu_custom_call" | custom-call | tf_op jit(solution)/shard_map/pallas_call | solution.py:755
  75.6 2.2 %shard_map.93 = (bf16[16,128,128]{2,1,0:T(8,128)(2,1)}, bf16[16,128,128]{2,1,0:T(8,128)(2,1)}, f32[3,3,4,8]{3,2,1,0:T(4,128)}, f32[3,3,4,16]{3,2,1,0:T(4,128)}, f32[3,3,8,8]{3,2,1,0:T(8,128)}) custom-call(bf16[16,128,128]{2,1,0:T(8,128)(2,1)} %get-tuple-element.15.refs_0_, bf16[16,128,128]{2,1,0:T(8,128)(2,1)} %get-tuple-element.16.refs_1_, ...), custom_call_target="tpu_custom_call" | custom-call | tf_op jit(solution)/shard_map/pallas_call | solution.py:829

commit v3 on v2

--- a/solution.py
+++ b/solution.py
@@ -164,7 +164,7 @@
 
 
 def sigmoid(value):
-    return 1.0 / (1.0 + jnp.exp(-value))
+    return 0.5 + 0.5 * jnp.tanh(0.5 * value)
 
 
 def pack_own(w_in, w_down, w_up, wide, own):
@@ -179,20 +179,19 @@
     own[...] = wide[...].astype(BF16)
 
 
-def columns(rows, first, width):
-    lane = lax.broadcasted_iota(jnp.int32, (128, width), 0)
-    wanted = lax.broadcasted_iota(jnp.int32, (128, width), 1) + first
+def lanes(block, first, count):
+    lane = lax.broadcasted_iota(jnp.int32, (count, 128), 1)
+    wanted = lax.broadcasted_iota(jnp.int32, (count, 128), 0) + first
     return lax.dot_general(
-        rows, (lane == wanted).astype(F32), (((1,), (0,)), ((), ())),
+        (lane == wanted).astype(F32), block, (((1,), (1,)), ((), ())),
         precision=lax.Precision.HIGHEST, preferred_element_type=F32,
     )
 
 
-def take_share(total, band, grad_in, grad_down, grad_up):
-    into = columns(total[0:40], band * 8, 8)
-    down = columns(total[DOWN_AT : DOWN_AT + 72], lax.rem(band, 8) * 16, 16)
-    up = columns(total[UP_AT : UP_AT + 72], band * 8, 8)
-    down = jnp.where(band < 8, down[0:36], down[36:72])
+def take_share(share, band, grad_in, grad_down, grad_up):
+    into = lanes(share[IN, 0:8], 0, 40)
+    down = lanes(share[DOWN, 0:16], 36 * lax.div(band, 8), 40)
+    up = lanes(share[UP, 0:8], 0, 72)
     for tap in range(9):
         j, l = tap // 3, tap % 3
         grad_in[j, l] = into[4 * tap : 4 * tap + 4]
@@ -282,12 +281,13 @@
 
 class Reduce:
     def __init__(self, job, parts, buffers, sems, scale):
-        first, count, self.main = JOBS[job]
-        self.rows = pl.ds(first, count)
+        first, self.count, self.main = JOBS[job]
+        self.rows = pl.ds(first, self.count)
+        self.job, self.width = job, 16 if job == DOWN else 8
         self.parts = parts
         (
             self.from_core, self.heavy_out, self.heavy_in, self.sums, self.light_out, self.light_in,
-            self.column, self.z_out, self.z_in, self.done, self.total, self.direct_out, self.direct_in,
+            self.column, self.z_out, self.z_in, self.done, self.share, self.direct_out, self.direct_in,
         ) = buffers
         self.sems = [sem.at[job] for sem in sems]
         self.scale = scale
@@ -368,10 +368,15 @@
             self.sems[6].at[0], self.sems[7].at[slot], device(self.x, self.y, self.z, 1 - self.core),
         )
 
+    def columns_of(self, x, core):
+        band = lax.rem(x * 4 + lax.div(self.z, 8) * 2 + core, 128 // self.width)
+        return pl.ds(pl.multiple_of(band * self.width, 8), self.width)
+
     def spread(self, count=7):
         return [
             remote(
-                self.done.at[self.rows], self.total.at[self.rows],
+                self.done.at[self.job, self.columns_of(on_ring(self.x, by, 4), lax.rem(self.core + swap, 2))],
+                self.share.at[self.job, pl.ds(0, self.width)],
                 self.sems[8].at[2 * by + swap], self.sems[9].at[0],
                 device(on_ring(self.x, by, 4), self.y, self.z, lax.rem(self.core + swap, 2)),
             )
@@ -422,10 +427,9 @@
                 for slot in range(15):
                     self.from_ring(slot).wait_recv()
                     total += self.z_in[slot, rows].astype(F32)
-                total = total * self.scale
-                self.done[rows] = total
+                self.done[self.job, :, 0 : self.count] = (total * self.scale).T
                 every(self.spread(), "start")
-                self.total[rows] = total
+                self.share[self.job, 0 : self.width] = self.done[self.job, self.columns_of(self.x, self.core)]
 
         if stage == 5:
             when(jnp.logical_not(self.holder), lambda: every(self.spread(1), "wait_recv"))
@@ -481,13 +485,15 @@
     w_in,
     w_down,
     w_up,
-    output,
-    input_grad,
+    output_far,
+    input_grad_far,
     grad_in,
     grad_down,
     grad_up,
     own,
     own_wide,
+    output,
+    input_grad,
     frames,
     cotangent,
     frames_above,
@@ -512,6 +518,8 @@
     win,
     wdn,
     wup,
+    sup,
+    turned_frames,
     fine,
     down,
     up,
@@ -531,6 +539,10 @@
         pltpu.make_async_copy(cotangent_far, cotangent, load_sem.at[1]),
     ]
     every(loads, "start")
+    stores = [
+        pltpu.make_async_copy(output, output_far, load_sem.at[2]),
+        pltpu.make_async_copy(input_grad, input_grad_far, load_sem.at[3]),
+    ]
     gathers = [Gather(job, own, full, gather_sems) for job in range(3)]
     reduces = [Reduce(job, parts, buffers, reduce_sems, scale) for job in range(3)]
 
@@ -552,6 +564,7 @@
 
     all_there = greet()
     pack_own(w_in, w_down, w_up, own_wide, own)
+    buffers[9][...] = jnp.zeros((3, 128, 128), F32)
     wide[:, 0:8] = jnp.zeros((23, 8, 128), F32)
     wide[:, 136:144] = jnp.zeros((23, 8, 128), F32)
     shifted[:, 0:8] = jnp.zeros((9, 8, 128), F32)
@@ -559,6 +572,13 @@
     shifted_wide[:, 64:72] = jnp.zeros((9, 8, 256), F32)
     every(loads, "wait")
     spread_columns(frames, 4, wide, fx, 4)
+
+    def turn(j, pair):
+        rows = flat(fx[3 + j + 2 * pair : 5 + j + 2 * pair])
+        turned_frames[512 * j : 512 * j + 512, 128 * pair : 128 * pair + 128] = rows.T
+
+    for pair in range(8):
+        turn(1, pair)
     all_there()
     for job in range(3):
         gathers[job].step(0)
@@ -580,29 +600,15 @@
     when(under_top, lambda: every(upward, "start"))
     gathers[IN].step(2)
     gathers[DOWN].step(2)
+    for pair in range(7):
+        turn(0, pair + 1)
+        turn(2, pair)
     spread_columns(cotangent, 3, wide, c3, 3)
     gathers[IN].step(3)
     gathers[UP].step(2)
     gathers[DOWN].step(3)
     gathers[IN].step(4)
-    unpack_in(full, win)
-    stack_in(win, fine, back_fine)
-    gathers[UP].step(3)
-    gathers[DOWN].step(4)
-    unpack_down(full, wdn)
-    stack_down(wdn, down, back_down)
-    gathers[UP].step(4)
-    unpack_up(full, wup)
-    stack_up(wup, up, back_up)
-
-    when(under_top, lambda: every(downward, "wait_recv"))
-    when(over_bottom, lambda: every(upward, "wait_recv"))
-    spread_columns(frames_above, 2, wide, fx, 4)
-    spread_columns(frames_below, 20, wide, fx, 4)
-    spread_columns(cotangent_above, 2, wide, c3, 3)
-    spread_columns(cotangent_below, 19, wide, c3, 3)
-
-    for first, count in ((2, 7), (9, 6), (15, 6)):
+    def fine_rows(first, count):
         pre = sum(matmul(flat(fx[first + j : first + j + count]), fine[j]) for j in range(3))
         gate = sigmoid(pre)
         hidden = (pre * gate).reshape(count, 64, 256)
@@ -617,6 +623,25 @@
             if 3 <= i < 19:
                 slopes[i - 3] = slope[row]
 
+    unpack_in(full, win)
+    stack_in(win, fine, back_fine)
+    fine_rows(4, 7)
+    gathers[UP].step(3)
+    gathers[DOWN].step(4)
+    unpack_down(full, wdn)
+    stack_down(wdn, down, back_down)
+    fine_rows(11, 7)
+
+    when(under_top, lambda: every(downward, "wait_recv"))
+    when(over_bottom, lambda: every(upward, "wait_recv"))
+    spread_columns(frames_above, 2, wide, fx, 4)
+    spread_columns(frames_below, 20, wide, fx, 4)
+    spread_columns(cotangent_above, 2, wide, c3, 3)
+    spread_columns(cotangent_below, 19, wide, c3, 3)
+
+    fine_rows(2, 2)
+    fine_rows(18, 3)
+
     @pl.when(top)
     def _():
         h3[1, 0] = jnp.zeros((64, 384), BF16)
@@ -633,6 +658,16 @@
     shifted_wide[:, 0:64] = coarse
     coarse2[:, :, 0:256] = coarse.astype(BF16)
     coarse2[:, :, 256:512] = shifted_wide[:, 1:65].astype(BF16)
+    turned = flat(coarse2[0:8, :, 0:256]).T
+    for j, (a, b) in enumerate(views):
+        found = matmul(turned, flat(c3[a : a + 8, b]))
+        for slot in range(3):
+            sup[3 * (2 - j) + 2 - slot] = found[:, slot * 128 : slot * 128 + 128].astype(BF16)
+    pack_up(parts, sup)
+    reduces[UP].step(0)
+    gathers[UP].step(4)
+    unpack_up(full, wup)
+    stack_up(wup, up, back_up)
     back = sum(matmul_t(flat(c3[a : a + 9, b]), back_up[j]) for j, (a, b) in enumerate(views))
     grad = (back * (gate * (1.0 + pre * (1.0 - gate)))).reshape(9, 64, 256)
     shifted_wide[:, 0:64] = grad
@@ -644,18 +679,11 @@
         coarse2[8] = jnp.zeros((64, 512), BF16)
         grad2[8] = jnp.zeros((64, 512), BF16)
 
-    turned = flat(coarse2[0:8, :, 0:256]).T
-    for j, (a, b) in enumerate(views):
-        found = matmul(turned, flat(c3[a : a + 8, b]))
-        for slot in range(3):
-            wup[3 * (2 - j) + 2 - slot] = found[:, slot * 128 : slot * 128 + 128].astype(BF16)
-    pack_up(parts, wup)
-    reduces[UP].step(0)
     turned = flat(grad2[0:8, :, 0:256]).T
     for j, (a, b) in enumerate(views):
         found = matmul(turned, flat(h3[a : a + 8, b]))
         for slot in range(3):
-            wdn[3 * j + slot] = found[:, slot * 128 : slot * 128 + 128].T.astype(BF16)
+            wdn[3 * j + slot] = found[:, slot * 128 : slot * 128 + 128].astype(BF16).T
     pack_down(parts, wdn)
     reduces[DOWN].step(0)
     reduces[UP].step(1)
@@ -687,12 +715,14 @@
     when(under_top, lambda: every(grad_up_copy, "start"))
 
     reduces[DOWN].step(1)
-    turned = flat(gx[1:17, :, 128:384]).T
+    turn(0, 0)
+    turn(2, 7)
+    found = matmul(turned_frames[...], flat(gx[1:17, :, 128:384]))
     for j in range(3):
-        found = matmul(turned, flat(fx[3 + j : 19 + j]))
         for l in range(3):
-            both = found[0:128, l * 128 : l * 128 + 128] + found[128:256, (l + 1) * 128 : (l + 2) * 128]
-            win[3 * j + l] = both.T.astype(BF16)
+            at = 512 * j + 128 * l
+            both = found[at : at + 128, 0:128] + found[at + 128 : at + 256, 128:256]
+            win[3 * j + l] = both.astype(BF16)
     pack_in(parts, win)
     reduces[IN].step(0)
     reduces[UP].step(2)
@@ -708,6 +738,7 @@
         mix(2 * t, even[64 * t : 64 * t + 64])
         mix(2 * t + 1, odd[64 * t : 64 * t + 64])
     output[...] = (frames[...].astype(F32) + mixed[...]).astype(BF16)
+    stores[0].start()
     reduces[DOWN].step(2)
     reduces[UP].step(3)
     reduces[IN].step(2)
@@ -732,12 +763,14 @@
         for row in range(8):
             mix(first + row, back[64 * row : 64 * row + 64])
     input_grad[...] = (cotangent[...].astype(F32) + mixed[...]).astype(BF16)
+    stores[1].start()
     for job in (UP, DOWN, IN):
         reduces[job].step(4)
     for job in (UP, DOWN, IN):
         reduces[job].step(5)
 
     take_share(buffers[10], band, grad_in, grad_down, grad_up)
+    every(stores, "wait")
     for job in range(3):
         gathers[job].step(5)
         reduces[job].step(6)
@@ -762,10 +795,12 @@
             jax.ShapeDtypeStruct((3, 3, 8, 8), F32),
         ),
         in_specs=[far, far, spec, spec, spec],
-        out_specs=(spec,) * 5,
+        out_specs=(far, far, spec, spec, spec),
         scratch_shapes=[
             vmem((PACK, 128), BF16),
             vmem((PACK, 128), F32),
+            vmem((16, 128, 128), BF16),
+            vmem((16, 128, 128), BF16),
             vmem((16, 128, 128), BF16),
             vmem((16, 128, 128), BF16),
             vmem((2, 128, 128), BF16),
@@ -790,6 +825,8 @@
             vmem((9, 128, 128), BF16),
             vmem((9, 128, 256), BF16),
             vmem((9, 256, 128), BF16),
+            vmem((9, 256, 128), BF16),
+            vmem((1536, 1024), BF16),
             vmem((3, 512, 256), BF16),
             vmem((3, 384, 256), BF16),
             vmem((3, 512, 256), BF16),
@@ -805,13 +842,13 @@
             vmem((PACK, 128), F32),
             vmem((PACK, 128), BF16),
             vmem((15, PACK, 128), BF16),
-            vmem((PACK, 128), F32),
-            vmem((PACK, 128), F32),
+            vmem((3, 128, 128), F32),
+            vmem((3, 16, 128), F32),
             vmem((16, DOWN_AT, 128), BF16),
             vmem((16, DOWN_AT, 128), BF16),
         ]
         + [dma((3, count)) for count in gather_counts + reduce_counts]
-        + [dma((6,)), dma((6,)), dma((2,))],
+        + [dma((6,)), dma((6,)), dma((4,))],
         compiler_params=pltpu.CompilerParams(
             collective_id=0, has_side_effects=True, vmem_limit_bytes=56 << 20
         ),

time: 78.1 us -> 76.2 us (0.976)
  the two profiles are of different devices: /device:TPU:3 before, /device:TPU:1 now
where the time goes in v3:
time: 76.2 us; the launch traced here: 75.5 us
  Pallas kernels  74.8 us (98%)
    pallas_call x1, Pallas kernels, whole(): pl.pallas_call(functools.partial(whole_kernel, scale), out_shape=(jax.Sha...  72.6 us
    pallas_call x1, Pallas kernels, hand_on(): pl.pallas_call(hand_on_kernel, out_shape=tuple((jax.ShapeDtypeStruct(arra...  2.24 us

profile of v3, /device:TPU:1, one launch (start us, length us, event | category | flops | bytes accessed | tf_op | source)
XLA Modules:
  0.0 75.5 jit_solution(3306281576322870764)
XLA Ops:
  0.6 72.6 %shard_map.92 = (bf16[16,128,128]{2,1,0:T(8,128)(2,1)}, bf16[16,128,128]{2,1,0:T(8,128)(2,1)}, f32[3,3,4,8]{3,2,1,0:T(4,128)}, f32[3,3,4,16]{3,2,1,0:T(4,128)}, f32[3,3,8,8]{3,2,1,0:T(8,128)}) custom-call(bf16[16,128,128]{2,1,0:T(8,128)(2,1)} %bitcast.4, bf16[16,128,128]{2,1,0:T(8,128)(2,1)} %bitcast.5, bf16[3,3,4,128]{3,2,1,0:T(4,128)(2,1)} %w_in.1, ...), custom_call_target="tpu_custom_call" | custom-call | tf_op jit(solution)/shard_map/pallas_call | solution.py:788
  73.2 2.2 %shard_map.93 = (bf16[16,128,128]{2,1,0:T(8,128)(2,1)}, bf16[16,128,128]{2,1,0:T(8,128)(2,1)}, f32[3,3,4,8]{3,2,1,0:T(4,128)}, f32[3,3,4,16]{3,2,1,0:T(4,128)}, f32[3,3,8,8]{3,2,1,0:T(8,128)}) custom-call(bf16[16,128,128]{2,1,0:T(8,128)(2,1)} %get-tuple-element.15.refs_0_, bf16[16,128,128]{2,1,0:T(8,128)(2,1)} %get-tuple-element.16.refs_1_, ...), custom_call_target="tpu_custom_call" | custom-call | tf_op jit(solution)/shard_map/pallas_call | solution.py:866

commit v4 on v3

--- a/solution.py
+++ b/solution.py
@@ -17,6 +17,7 @@
 HOPS = (1, -1, 2, -2, 3, -3, 4)
 JOBS = ((0, 48, "x"), (48, 80, "y"), (128, 80, "x"))
 IN, DOWN, UP = 0, 1, 2
+AT_ONCE = (IN, DOWN, UP)
 
 
 def place():
@@ -291,7 +292,9 @@
         ) = buffers
         self.sems = [sem.at[job] for sem in sems]
         self.scale = scale
-        self.at_once = job == IN
+        self.at_once = job in AT_ONCE
+        if self.at_once:
+            self.main = "x"
         self.x, self.y, self.z, self.core = place()
         self.carried = self.x + 4 * self.core
         self.holder = lax.rem(self.z, 8) == self.carried
@@ -326,7 +329,7 @@
     def direct(self, slot):
         where = device(on_ring(self.x, slot // 4, 4), on_ring(self.y, slot % 4, 4), self.z, self.core)
         return remote(
-            self.direct_out.at[slot], self.direct_in.at[slot], self.sems[10].at[slot], self.sems[11].at[slot], where
+            self.direct_out.at[slot, self.rows], self.direct_in.at[slot, self.rows], self.sems[10].at[slot], self.sems[11].at[slot], where
         )
 
     def step_direct(self, stage):
@@ -338,14 +341,14 @@
                 for turn in (2, 1, 3, 0):
                     if by or turn:
                         slot = 4 * by + turn
-                        self.direct_out[slot] = self.sums[on_ring(self.y, turn, 4), rows].astype(BF16)
+                        self.direct_out[slot, rows] = self.sums[on_ring(self.y, turn, 4), rows].astype(BF16)
                         self.direct(slot).start()
             self.column[rows] = self.sums[self.y, rows]
         if stage == 3:
             total = self.column[rows]
             for slot in (4, 12, 1, 3, 8, 2, 5, 7, 13, 15, 6, 9, 11, 14, 10):
                 self.direct(slot).wait_recv()
-                total += self.direct_in[slot].astype(F32)
+                total += self.direct_in[slot, rows].astype(F32)
             self.column[rows] = total
             self.send_to_holders(total)
 
@@ -600,13 +603,13 @@
     when(under_top, lambda: every(upward, "start"))
     gathers[IN].step(2)
     gathers[DOWN].step(2)
+    gathers[UP].step(2)
+    spread_columns(cotangent, 3, wide, c3, 3)
+    gathers[IN].step(3)
+    gathers[DOWN].step(3)
     for pair in range(7):
         turn(0, pair + 1)
         turn(2, pair)
-    spread_columns(cotangent, 3, wide, c3, 3)
-    gathers[IN].step(3)
-    gathers[UP].step(2)
-    gathers[DOWN].step(3)
     gathers[IN].step(4)
     def fine_rows(first, count):
         pre = sum(matmul(flat(fx[first + j : first + j + count]), fine[j]) for j in range(3))
@@ -844,8 +847,8 @@
             vmem((15, PACK, 128), BF16),
             vmem((3, 128, 128), F32),
             vmem((3, 16, 128), F32),
-            vmem((16, DOWN_AT, 128), BF16),
-            vmem((16, DOWN_AT, 128), BF16),
+            vmem((16, PACK, 128), BF16),
+            vmem((16, PACK, 128), BF16),
         ]
         + [dma((3, count)) for count in gather_counts + reduce_counts]
         + [dma((6,)), dma((6,)), dma((4,))],

time: 76.2 us -> 72.3 us (0.949)
  Pallas kernels: 74.8 us -> 71.2 us
    pallas_call x1, Pallas kernels: 72.6 us -> 68.9 us  [whole(): pl.pallas_call(functools.partial(whole_kernel, scale), out_shape=(jax.Sha...]
where the time goes in v4:
time: 72.3 us; the launch traced here: 71.8 us
  Pallas kernels  71.2 us (98%)
    pallas_call x1, Pallas kernels, whole(): pl.pallas_call(functools.partial(whole_kernel, scale), out_shape=(jax.Sha...  68.9 us
    pallas_call x1, Pallas kernels, hand_on(): pl.pallas_call(hand_on_kernel, out_shape=tuple((jax.ShapeDtypeStruct(arra...  2.24 us

profile of v4, /device:TPU:1, one launch (start us, length us, event | category | flops | bytes accessed | tf_op | source)
XLA Modules:
  0.0 71.8 jit_solution(16754126301116611736)
XLA Ops:
  0.6 68.9 %shard_map.92 = (bf16[16,128,128]{2,1,0:T(8,128)(2,1)}, bf16[16,128,128]{2,1,0:T(8,128)(2,1)}, f32[3,3,4,8]{3,2,1,0:T(4,128)}, f32[3,3,4,16]{3,2,1,0:T(4,128)}, f32[3,3,8,8]{3,2,1,0:T(8,128)}) custom-call(bf16[16,128,128]{2,1,0:T(8,128)(2,1)} %bitcast.4, bf16[16,128,128]{2,1,0:T(8,128)(2,1)} %bitcast.5, bf16[3,3,4,128]{3,2,1,0:T(4,128)(2,1)} %w_in.1, ...), custom_call_target="tpu_custom_call" | custom-call | tf_op jit(solution)/shard_map/pallas_call | solution.py:791
  69.6 2.2 %shard_map.93 = (bf16[16,128,128]{2,1,0:T(8,128)(2,1)}, bf16[16,128,128]{2,1,0:T(8,128)(2,1)}, f32[3,3,4,8]{3,2,1,0:T(4,128)}, f32[3,3,4,16]{3,2,1,0:T(4,128)}, f32[3,3,8,8]{3,2,1,0:T(8,128)}) custom-call(bf16[16,128,128]{2,1,0:T(8,128)(2,1)} %get-tuple-element.15.refs_0_, bf16[16,128,128]{2,1,0:T(8,128)(2,1)} %get-tuple-element.16.refs_1_, ...), custom_call_target="tpu_custom_call" | custom-call | tf_op jit(solution)/shard_map/pallas_call | solution.py:869
